TPU v7x, 1024 devices: a whole 4x4x32 slice. The times are simulated.
1024 devices in a mesh: wide: 64 (over z, core), pan: 4 (over x), rep: 4 (over y).
Axes of the slice: x: 4, y: 4, z: 32, core: 2. Of those that a mesh axis runs over, the one named last changes fastest.
Arguments:
- amplitudes: float32 [8, 1536, 1536], P(None, 'wide', ('pan', 'rep')), may hold values from -0.15625 to 0.15625
- integrals: float32 [8, 1536, 1536], P(None, ('pan', 'rep'), 'wide'), may hold values from -6 to 6
- pair_energies: float32 [8, 1536], replicated, may hold values from 0.5 to 4
- block_sizes: int32 [8], replicated, may hold values from 768 to 1536, as said below
Outputs:
- residual: float32 [8, 1536, 1536], P(None, 'wide')
- update: float32 [8, 1536, 1536], P(None, 'wide')
Inputs may be any that keep to these rules, and one draw needn't show every extreme that they name: Block h holds block_sizes[h] live ov pairs, the leading slots of its 1536; some block holds exactly 1536.
All inputs are finite; a program needn't handle non-finite values.
Results may differ from a plain program's by a relative error of at most 0.000071.
Values sent between devices are 32-bit elements; how exact they have to be, the bound alone decides.
A program may use at most 64 MiB of HBM per device.

v0:
```python
import jax
import jax.numpy as jnp
from jax import lax
from jax.sharding import PartitionSpec as P


def contract(first_factor, second_factor):
    return jnp.einsum("hpk,hkq->hpq", first_factor, second_factor, precision=lax.Precision.HIGHEST)


def shards(amplitudes, integrals, pair_energies, block_sizes):
    row_count = amplitudes.shape[1]
    sum_count = amplitudes.shape[2]
    slot_count = pair_energies.shape[1]
    position = jnp.arange(slot_count, dtype=jnp.int32)
    live_mask = (position[None, :] < block_sizes[:, None]).astype(jnp.float32)
    row_start = lax.axis_index("wide") * row_count
    sum_start = lax.axis_index(("pan", "rep")) * sum_count
    row_live = lax.dynamic_slice_in_dim(live_mask, row_start, row_count, 1)
    sum_live = lax.dynamic_slice_in_dim(live_mask, sum_start, sum_count, 1)
    amp_live = amplitudes * row_live[:, :, None] * sum_live[:, None, :]
    int_live = integrals * sum_live[:, :, None] * row_live[:, None, :]
    partial_rows = contract(amp_live, lax.all_gather(int_live, "wide", axis=2, tiled=True))
    cycle_rows = lax.psum(partial_rows, ("pan", "rep"))
    flipped = lax.all_to_all(cycle_rows, "wide", split_axis=2, concat_axis=1, tiled=True)
    residual = cycle_rows + jnp.swapaxes(flipped, 1, 2)
    energy_rows = lax.dynamic_slice_in_dim(pair_energies, row_start, row_count, 1)
    denominator = energy_rows[:, :, None] + pair_energies[:, None, :]
    update = -residual / denominator
    return (residual, update)


def solution(mesh):
    in_specs = (P(None, "wide", ("pan", "rep")), P(None, ("pan", "rep"), "wide"), P(), P())
    out_specs = (P(None, "wide", None), P(None, "wide", None))
    return jax.shard_map(shards, mesh=mesh, in_specs=in_specs, out_specs=out_specs, check_vma=False)
```

profile of v0, /device:TPU:1, one launch (start us, length us, event | category | flops | bytes accessed | tf_op | source)
XLA Modules:
  0.0 508.9 jit_solution(2288898712164406750)
XLA Ops:
  7.2 0.0 all-gather.2.cloned.1.call-start
  7.2 0.7 fusion.5
  7.9 0.1 constant_dynamic-slice_fusion.1
  8.0 0.1 constant_dynamic-slice_fusion.2
  8.1 1.6 multiply_multiply_fusion
  9.7 0.0 all-gather.2.cloned.1.call-update
  9.7 0.0 all-reduce.2.cloned.1.call-start
  9.8 152.3 %all-gather.2.cloned.1.call-done = f32[8,96,1536]{1,2,0:T(8,128)} async-done(((f32[8,96,24]{1,2,0:T(8,128)}), f32[8,96,1536]{1,2,0:T(8,128)}) %all-gather.2.cloned.1.call-update) | async-done | bytes 4718608 | tf_op jit(solution)/shard_map/all_gather | solution.py:23
  162.1 8.3 %fusion = f32[8,24,1536]{2,1,0:T(8,128)} fusion(f32[8,96,1536]{1,2,0:T(8,128)} %all-gather.2.cloned.1.call-done, f32[8,24,96]{2,1,0:T(8,128)} %param.4, f32[8,96]{1,0:T(8,128)S(1)} %constant_dynamic-slice_fusion.1, f32[8,24]{1,0:T(8,128)S(1)} %constant_dynamic-slice_fusion.2), kind=kOutput, calls=%fused_computation.3 | convolution fusion | flops 339775488 | bytes 5975808 | tf_op jit(solution)/shard_map/hpk,hkq->hpq/dot_general | solution.py:8
  170.5 0.0 all-reduce.2.cloned.1.call-update
  170.5 148.1 %all-reduce.2.cloned.1.call-done = f32[8,24,1536]{2,1,0:T(8,128)} async-done(((f32[8,24,1536]{2,1,0:T(8,128)}), f32[8,24,1536]{2,1,0:T(8,128)}) %all-reduce.2.cloned.1.call-update) | async-done | bytes 1179664 | tf_op jit(solution)/shard_map/psum | solution.py:24
  318.6 4.9 copy.8
  323.5 7.2 %reshape.11 = f32[64,1,4608]{2,1,0:T(1,128)} reshape(f32[1536,8,24]{2,1,0:T(8,128)} %bitcast.15) | data formatting | bytes 2359296
  330.7 0.0 copy-start.1
  330.7 25.4 %all-to-all-start = ((f32[64,1,4608]{2,1,0:T(1,128)}), f32[64,1,4608]{2,1,0:T(1,128)S(1)}, u32[]{:S(2)}, u32[]{:S(2)}) async-start(f32[64,1,4608]{2,1,0:T(1,128)} %reshape.11), calls=%async_computation | async-start | bytes 2359296 | tf_op jit(solution)/shard_map/all_to_all | solution.py:25
  356.1 0.0 copy-done.1
  356.2 0.1 constant_dynamic-slice_fusion
  356.2 119.2 %all-to-all-done = f32[64,1,4608]{2,1,0:T(1,128)S(1)} async-done(((f32[64,1,4608]{2,1,0:T(1,128)}), f32[64,1,4608]{2,1,0:T(1,128)S(1)}, u32[]{:S(2)}, u32[]{:S(2)}) %all-to-all-start) | async-done | bytes 1179680 | tf_op jit(solution)/shard_map/all_to_all | solution.py:25
  475.4 0.5 broadcast.7
  475.9 3.4 reduce
  479.4 6.2 %reshape.12 = f32[1536,8,24]{2,1,0:T(8,128)} reshape(f32[64,4608]{1,0:T(8,128)S(1)} %reduce) | data formatting | bytes 2359296
  485.6 9.1 %copy.10 = f32[8,64,24,24]{2,1,3,0:T(8,128)} copy(f32[8,64,24,24]{2,0,3,1:T(8,128)} %bitcast.14) | data formatting | bytes 2359296 | tf_op jit(solution)/shard_map/all_to_all | solution.py:25
  494.7 0.0 copy-start
  494.7 5.6 %all_to_all.16 = f32[8,1536,24]{1,2,0:T(8,128)S(1)} reshape(f32[8,64,24,24]{2,1,3,0:T(8,128)} %copy.10) | data formatting | bytes 2359296 | tf_op jit(solution)/shard_map/all_to_all | solution.py:25
  500.3 0.0 copy-done
  500.3 1.7 add_divide_fusion
Async XLA Ops:
  7.2 155.0 %all-gather.2.cloned.1.call-start = ((), (), s32[]{:S(2)}) async-start(), calls=%async_computation.1 | async-start | bytes 6389760 | tf_op jit(solution)/shard_map/all_gather | solution.py:23
  9.7 308.8 %all-reduce.2.cloned.1.call-start = ((), (), s32[]{:S(2)}) async-start(), calls=%async_computation.2 | async-start | bytes 2359296 | tf_op jit(solution)/shard_map/psum | solution.py:24
  330.7 25.5 %copy-start.1 = (f32[8,1536]{1,0:T(8,128)S(1)}, f32[8,1536]{1,0:T(8,128)}, u32[]{:S(2)}) copy-start(f32[8,1536]{1,0:T(8,128)} %param.6) | copy-start | bytes 147460
  330.7 144.7 %all-to-all-start = ((f32[64,1,4608]{2,1,0:T(1,128)}), f32[64,1,4608]{2,1,0:T(1,128)S(1)}, u32[]{:S(2)}, u32[]{:S(2)}) async-start(f32[64,1,4608]{2,1,0:T(1,128)} %reshape.11), calls=%async_computation | async-start | bytes 2359296 | tf_op jit(solution)/shard_map/all_to_all | solution.py:25
  494.7 5.6 %copy-start = (f32[8,24,1536]{2,1,0:T(8,128)S(1)}, f32[8,24,1536]{2,1,0:T(8,128)}, u32[]{:S(2)}) copy-start(f32[8,24,1536]{2,1,0:T(8,128)} %all-reduce.2.cloned.1.call-done) | copy-start | bytes 3538948
Sparse Core Ops, SparseCore 0:
  11.3 150.7 all-gather.1
  170.6 147.9 all-reduce.1
where the time goes:
time: 510 us; the launch traced here: 509 us
  waiting for transfers between devices  420 us (82%)
  local copies, waits for them, and re-layouts  33.8 us (7%)
  starting transfers between devices  25.5 us (5%)
  between operations  14.1 us (3%)
  matrix products  8.33 us (2%)
  other arithmetic  7.53 us (1%)
    all_gather x1, waiting for transfers between devices, shards(): lax.all_gather(int_live, 'wide', axis=2, tiled=True)  152 us
    psum x1, waiting for transfers between devices, shards(): cycle_rows = lax.psum(partial_rows, ('pan', 'rep'))  148 us
    all_to_all x1, waiting for transfers between devices, shards(): lax.all_to_all(cycle_rows, 'wide', split_axis=2, concat_axis=1, tiled=True)  119 us
    all_to_all x1, starting transfers between devices, shards(): lax.all_to_all(cycle_rows, 'wide', split_axis=2, concat_axis=1, tiled=True)  25.4 us
    all_to_all x3, local copies, waits for them, and re-layouts, shards(): lax.all_to_all(cycle_rows, 'wide', split_axis=2, concat_axis=1, tiled=True)  15.2 us
    unnamed x6, local copies, waits for them, and re-layouts  13.5 us
  transfers between devices with their start and end apart: 3, of which 3 were waited for; matrix products, arithmetic and copies ran while one was open for 0% of the time, Pallas kernels for 0%

commit v1 on v0

v1 whole, which is shorter than its diff:
```python
import jax
import jax.numpy as jnp
from jax import lax
from jax.experimental import pallas as pl
from jax.experimental.pallas import tpu as pltpu
from jax.sharding import PartitionSpec as P

MESH = pl.DeviceIdType.MESH


def cycle_kernel(
    sizes_ref, amp_ref, int_ref, out_ref,
    stage, held, amp_all, int_all, part, parts, block_out, block_in, rows_out,
    send1, recv1, send_a, recv_a, send_b, recv_b, send_c, recv_c,
    send3, recv3, send4, recv4, send5, recv5, send6, recv6, send7, recv7,
):
    wide, pan, rep = lax.axis_index("wide"), lax.axis_index("pan"), lax.axis_index("rep")
    z, core = wide // 2, wide % 2
    owner, layer = z // 4, z % 4
    band, rank = z // 8, z % 8

    def device(w, x, y):
        return {"wide": w, "pan": x, "rep": y}

    def remote(src, dst, ssem, rsem, to):
        return pltpu.make_async_remote_copy(
            src_ref=src, dst_ref=dst, send_sem=ssem, recv_sem=rsem,
            device_id=device(*to), device_id_type=MESH,
        )

    def is_me(to):
        return (to[0] == wide) & (to[1] == pan) & (to[2] == rep)

    def start(src, dst, ssem, rsem, to):
        me = is_me(to)

        @pl.when(me)
        def _():
            pltpu.make_async_copy(src, dst, rsem).start()

        @pl.when(jnp.logical_not(me))
        def _():
            remote(src, dst, ssem, rsem, to).start()

    def finish_send(src, dst, ssem, rsem, to):
        @pl.when(jnp.logical_not(is_me(to)))
        def _():
            remote(src, dst, ssem, rsem, to).wait_send()

    def arrived(dst, rsem):
        pltpu.make_async_copy(dst, dst, rsem).wait()

    row_at = wide * 24 + lax.broadcasted_iota(jnp.int32, (24, 96), 0)
    sum_at = (pan * 4 + rep) * 96 + lax.broadcasted_iota(jnp.int32, (24, 96), 1)
    stage[...] = jnp.zeros_like(stage)
    for h in range(8):
        live = (row_at < sizes_ref[h]) & (sum_at < sizes_ref[h])
        stage[h, 0:24, 0:96] = jnp.where(live, amp_ref[h], 0.0)
        stage[h, 24:48, 0:96] = jnp.where(live, int_ref[h], 0.0)

    slot1 = (rank % 4) * 2 + core
    sends1 = []
    for step in range(8):
        h = (owner + step) % 8
        to = (2 * (4 * h + band) + rank // 4, pan, rep)
        sends1.append((stage.at[h], held.at[slot1], send1.at[step], recv1.at[slot1], to))
        start(*sends1[-1])
    for i in range(8):
        arrived(held.at[i], recv1.at[i])

    sends2 = []
    for step in range(1, 4):
        y = (rep + step) % 4
        sends2.append((held.at[:, 0:24], amp_all.at[rep], send_a.at[step], recv_a.at[rep], (wide, pan, y)))
        remote(*sends2[-1]).start()
    sends2b = []
    for step in range(4):
        to = (2 * (4 * owner + (layer + step) % 4) + core, pan, layer)
        sends2b.append((held.at[:, 24:48], int_all.at[core, rep], send_b.at[step], recv_b.at[rep], to))
        start(*sends2b[-1])
    own_amp = pltpu.make_async_copy(held.at[:, 0:24], amp_all.at[rep], send_a.at[0])
    own_amp.start()
    sends2c = []
    for y in range(4):
        arrived(int_all.at[core, y], recv_b.at[y])
        sends2c.append((int_all.at[core, y], int_all.at[core, y], send_c.at[y], recv_c.at[y], (2 * z + 1 - core, pan, rep)))
        remote(*sends2c[-1]).start()
    own_amp.wait()
    for step in range(1, 4):
        y = (rep + step) % 4
        arrived(amp_all.at[y], recv_a.at[y])
    for y in range(4):
        arrived(int_all.at[1 - core, y], recv_c.at[y])

    for side in range(2):
        total = jnp.zeros((192, 192), jnp.float32)
        for y in range(4):
            total = total + lax.dot_general(
                amp_all[y].reshape(192, 128), int_all[side, y].reshape(192, 128),
                (((1,), (1,)), ((), ())), precision=lax.Precision.HIGHEST, preferred_element_type=jnp.float32,
            )
        part[:, 192 * side:192 * (side + 1)] = total
    sends3 = []
    for step in range(1, 4):
        x = (pan + step) % 4
        rows = part.at[pl.ds(pl.multiple_of(48 * x, 8), 48)]
        sends3.append((rows, parts.at[pan], send3.at[step], recv3.at[pan], (wide, x, rep)))
        remote(*sends3[-1]).start()
    parts[pan] = part[pl.ds(pl.multiple_of(48 * pan, 8), 48)]
    for step in range(1, 4):
        x = (pan + step) % 4
        arrived(parts.at[x], recv3.at[x])
    cycle = parts[0] + parts[1] + parts[2] + parts[3]

    flipped = jnp.concatenate([cycle, jnp.zeros((80, 384), jnp.float32)], axis=0).T
    block_out[...] = flipped.reshape(8, 48, 128)
    mine = 4 * core + pan
    sends4 = []
    for step in range(8):
        b = (mine + step) % 8
        to = (2 * (4 * owner + rep) + b // 4, b % 4, layer)
        sends4.append((block_out.at[b], block_in.at[mine], send4.at[step], recv4.at[mine], to))
        start(*sends4[-1])
    mirror = jnp.zeros((48, 384), jnp.float32)
    for b in range(8):
        arrived(block_in.at[b], recv4.at[b])
        widened = jnp.concatenate([block_in[b], jnp.zeros((48, 256), jnp.float32)], axis=1)
        mirror = mirror + (pltpu.roll(widened, 48 * b, 1) if b else widened)
    rows_out[...] = cycle + mirror

    columns = pl.ds(pl.multiple_of(384 * rep, 128), 384)
    sends5 = []
    for c in range(2):
        to = (2 * (8 * layer + 4 * core + pan) + c, (owner + layer) % 4, rep)
        sends5.append((rows_out.at[24 * c:24 * (c + 1)], out_ref.at[owner, :, columns], send5.at[c], recv5.at[owner // 4], to))
        start(*sends5[-1])

    first = (pan + 4 - band) % 4
    sends6 = []
    arrived(out_ref.at[first, :, columns], recv5.at[0])
    for step in range(1, 4):
        to = (wide, pan, (rep + step) % 4)
        here = out_ref.at[first, :, columns]
        sends6.append((here, here, send6.at[0, step], recv6.at[0, rep], to))
        remote(*sends6[-1]).start()
    arrived(out_ref.at[first + 4, :, columns], recv5.at[1])
    for step in range(1, 4):
        to = (wide, (pan + step) % 4, rep)
        here = out_ref.at[first + 4, :, columns]
        sends6.append((here, here, send6.at[1, step], recv6.at[1, pan], to))
        remote(*sends6[-1]).start()
    for step in range(1, 4):
        y = (rep + step) % 4
        arrived(out_ref.at[first, :, pl.ds(pl.multiple_of(384 * y, 128), 384)], recv6.at[0, y])
    sends7 = []
    for step in range(1, 4):
        to = (wide, (pan + step) % 4, rep)
        here = out_ref.at[first]
        sends7.append((here, here, send7.at[0, step], recv7.at[0, pan], to))
        remote(*sends7[-1]).start()
    for step in range(1, 4):
        x = (pan + step) % 4
        arrived(out_ref.at[(x + 4 - band) % 4 + 4, :, columns], recv6.at[1, x])
    for step in range(1, 4):
        to = (wide, pan, (rep + step) % 4)
        here = out_ref.at[4:8, :, columns]
        sends7.append((here, here, send7.at[1, step], recv7.at[1, rep], to))
        remote(*sends7[-1]).start()
    for step in range(1, 4):
        x = (pan + step) % 4
        arrived(out_ref.at[(x + 4 - band) % 4], recv7.at[0, x])
    for step in range(1, 4):
        y = (rep + step) % 4
        arrived(out_ref.at[4:8, :, pl.ds(pl.multiple_of(384 * y, 128), 384)], recv7.at[1, y])

    for args in sends1 + sends2b + sends4 + sends5:
        finish_send(*args)
    for args in sends2 + sends2c + sends3 + sends6 + sends7:
        remote(*args).wait_send()


def shards(amplitudes, integrals, pair_energies, block_sizes):
    vmem = pl.BlockSpec(memory_space=pltpu.VMEM)
    dma = pltpu.SemaphoreType.DMA
    residual = pl.pallas_call(
        cycle_kernel,
        out_shape=jax.ShapeDtypeStruct((8, 24, 1536), jnp.float32),
        in_specs=[pl.BlockSpec(memory_space=pltpu.SMEM), vmem, vmem],
        out_specs=vmem,
        scratch_shapes=[
            pltpu.VMEM((8, 48, 128), jnp.float32),
            pltpu.VMEM((8, 48, 128), jnp.float32),
            pltpu.VMEM((4, 8, 24, 128), jnp.float32),
            pltpu.VMEM((2, 4, 8, 24, 128), jnp.float32),
            pltpu.VMEM((192, 384), jnp.float32),
            pltpu.VMEM((4, 48, 384), jnp.float32),
            pltpu.VMEM((8, 48, 128), jnp.float32),
            pltpu.VMEM((8, 48, 128), jnp.float32),
            pltpu.VMEM((48, 384), jnp.float32),
            dma((8,)), dma((8,)),
            dma((4,)), dma((4,)), dma((4,)), dma((4,)), dma((4,)), dma((4,)),
            dma((4,)), dma((4,)), dma((8,)), dma((8,)), dma((2,)), dma((2,)),
            dma((2, 4)), dma((2, 4)), dma((2, 4)), dma((2, 4)),
        ],
        compiler_params=pltpu.CompilerParams(has_side_effects=True, vmem_limit_bytes=24 * 1024 * 1024),
        cost_estimate=pl.CostEstimate(flops=60_000_000, bytes_accessed=2_000_000, transcendentals=0),
    )(block_sizes, amplitudes, jnp.swapaxes(integrals, 1, 2))
    row_start = lax.axis_index("wide") * 24
    energy_rows = lax.dynamic_slice_in_dim(pair_energies, row_start, 24, 1)
    update = -residual / (energy_rows[:, :, None] + pair_energies[:, None, :])
    return (residual, update)


def solution(mesh):
    in_specs = (P(None, "wide", ("pan", "rep")), P(None, ("pan", "rep"), "wide"), P(), P())
    out_specs = (P(None, "wide", None), P(None, "wide", None))
    return jax.shard_map(shards, mesh=mesh, in_specs=in_specs, out_specs=out_specs, check_vma=False)
```

time: 510 us -> 132 us (0.26)
  waiting for transfers between devices: 420 us -> 0 us
  Pallas kernels: 0 us -> 126 us
  local copies, waits for them, and re-layouts: 33.8 us -> 3.53 us
  starting transfers between devices: 25.5 us -> 0 us
  between operations: 14.1 us -> 0.66 us
  matrix products: 8.33 us -> 0 us
  other arithmetic: 7.53 us -> 1.24 us
    all_gather x1 -> x0, waiting for transfers between devices: 152 us -> none  [shards(): lax.all_gather(int_live, 'wide', axis=2, tiled=True)]
    psum x1 -> x0, waiting for transfers between devices: 148 us -> none  [shards(): cycle_rows = lax.psum(partial_rows, ('pan', 'rep'))]
    pallas_call x0 -> x1, Pallas kernels: none -> 126 us  [shards(): pl.pallas_call(cycle_kernel, out_shape=jax.ShapeDtypeStruct((8, 24, 1536)...]
    all_to_all x1 -> x0, waiting for transfers between devices: 119 us -> none  [shards(): lax.all_to_all(cycle_rows, 'wide', split_axis=2, concat_axis=1, tiled=True)]
    all_to_all x1 -> x0, starting transfers between devices: 25.4 us -> none  [shards(): lax.all_to_all(cycle_rows, 'wide', split_axis=2, concat_axis=1, tiled=True)]
    all_to_all x3 -> x0, local copies, waits for them, and re-layouts: 15.2 us -> none  [shards(): lax.all_to_all(cycle_rows, 'wide', split_axis=2, concat_axis=1, tiled=True)]
    unnamed x6 -> x9, local copies, waits for them, and re-layouts: 13.5 us -> 3.45 us
    dot_general x1 -> x0, matrix products: 8.33 us -> none  [contract(): jnp.einsum('hpk,hkq->hpq', first_factor, second_factor, precision=lax.Pre...]
  transfers between devices with their start and end apart: 3 -> 0, of which waited for: 3 -> 0; matrix products, arithmetic and copies ran while one was open for 0% -> 0% of each run, Pallas kernels for 0% -> 0%
where the time goes in v1:
time: 132 us; the launch traced here: 131 us
  Pallas kernels  126 us (95%)
  local copies, waits for them, and re-layouts  3.53 us (3%)
    pallas_call x1, Pallas kernels, shards(): pl.pallas_call(cycle_kernel, out_shape=jax.ShapeDtypeStruct((8, 24, 1536)...  126 us
    unnamed x9, local copies, waits for them, and re-layouts  3.45 us

profile of v1, /device:TPU:1, one launch (start us, length us, event | category | flops | bytes accessed | tf_op | source)
XLA Modules:
  0.0 131.1 jit_solution(3086826058566309613)
XLA Ops:
  0.6 0.0 copy-start
  0.6 0.9 copy-done
  1.5 0.0 copy-start.1
  1.5 0.9 copy-done.1
  2.4 0.0 copy-start.2
  2.4 0.7 copy-done.2
  3.1 0.0 copy-start.3
  3.1 125.6 %shard_map.59 = f32[8,24,1536]{2,1,0:T(8,128)S(1)} custom-call(s32[8]{0:T(128)S(1)} %copy-done.2, f32[8,24,96]{2,1,0:T(8,128)S(1)} %copy-done, f32[8,24,96]{2,1,0:T(8,128)S(1)} %bitcast.1), custom_call_target="tpu_custom_call" | custom-call | flops 60000000 | bytes 2000000 | tf_op jit(solution)/shard_map/pallas_call | solution.py:185
  128.7 0.0 copy-done.3
  128.7 0.1 constant_dynamic-slice_fusion
  128.8 1.2 add_divide_fusion
  130.1 1.0 copy.7
Async XLA Ops:
  0.6 0.9 copy-start
  1.5 0.9 copy-start.1
  2.4 0.7 copy-start.2
  3.1 125.7 %copy-start.3 = (f32[8,1536]{1,0:T(8,128)S(1)}, f32[8,1536]{1,0:T(8,128)}, u32[]{:S(2)}) copy-start(f32[8,1536]{1,0:T(8,128)} %param.6) | copy-start | bytes 147460

commit v2 on v1

--- a/solution.py
+++ b/solution.py
@@ -9,9 +9,9 @@
 
 
 def cycle_kernel(
-    sizes_ref, amp_ref, int_ref, out_ref,
-    stage, held, amp_all, int_all, part, parts, block_out, block_in, rows_out,
-    send1, recv1, send_a, recv_a, send_b, recv_b, send_c, recv_c,
+    sizes_ref, amp_hbm, int_hbm, out_ref,
+    amp_ref, int_ref, stage, held_packed, held, amp_all, int_all, part, parts, block_out, block_in, rows_out,
+    load, send1, recv1, send_a, recv_a, send_b, recv_b, send_c, recv_c,
     send3, recv3, send4, recv4, send5, recv5, send6, recv6, send7, recv7,
 ):
     wide, pan, rep = lax.axis_index("wide"), lax.axis_index("pan"), lax.axis_index("rep")
@@ -50,37 +50,84 @@
     def arrived(dst, rsem):
         pltpu.make_async_copy(dst, dst, rsem).wait()
 
-    row_at = wide * 24 + lax.broadcasted_iota(jnp.int32, (24, 96), 0)
-    sum_at = (pan * 4 + rep) * 96 + lax.broadcasted_iota(jnp.int32, (24, 96), 1)
-    stage[...] = jnp.zeros_like(stage)
+    sends1, sends2, sends2b, sends2c, sends3, sends4, sends5, sends6, sends7 = [[] for _ in range(9)]
+
+    def drain():
+        for args in sends1 + sends2b + sends4 + sends5:
+            finish_send(*args)
+        for args in sends2 + sends2c + sends3 + sends6 + sends7:
+            remote(*args).wait_send()
+
+    loads = [
+        pltpu.make_async_copy(amp_hbm, amp_ref, load.at[0]),
+        pltpu.make_async_copy(int_hbm, int_ref, load.at[1]),
+    ]
+    for copy in loads:
+        copy.start()
+
+    first = (pan + 4 - z % 4) % 4
+    callers = [(2 * (8 * layer + 4 * core + i // 2) + i % 2, pan, rep) for i in range(8)]
+    callers += [(wide, pan, (rep + step) % 4) for step in range(1, 4)]
+    callers += [(wide, (pan + step) % 4, rep) for step in range(1, 4)]
+    callers += [(2 * z + 1 - core, pan, rep)]
+    callers += [(2 * (4 * owner + rep) + core, pan, y) for y in range(4)]
+    callers += [(2 * (4 * owner + rep) + b // 4, b % 4, layer) for b in range(8)]
+    callers += [(2 * (4 * (first + 4 * i) + band) + rank // 4, z % 4, rep) for i in range(2)]
+    barrier = pltpu.get_barrier_semaphore()
+    for to in callers:
+        pl.semaphore_signal(barrier, inc=1, device_id=device(*to), device_id_type=MESH)
+
+    row_at = wide * 24 + lax.broadcasted_iota(jnp.int32, (24, 128), 0)
+    lane = lax.broadcasted_iota(jnp.int32, (24, 128), 1)
+    sum_at = (pan * 4 + rep) * 96 + lane
+    lane8 = lane[0:8]
+    for copy in loads:
+        copy.wait()
     for h in range(8):
-        live = (row_at < sizes_ref[h]) & (sum_at < sizes_ref[h])
-        stage[h, 0:24, 0:96] = jnp.where(live, amp_ref[h], 0.0)
-        stage[h, 24:48, 0:96] = jnp.where(live, int_ref[h], 0.0)
+        live = (row_at < sizes_ref[h]) & (sum_at < sizes_ref[h]) & (lane < 96)
+        tails = []
+        for side, ref in enumerate((amp_ref, int_ref)):
+            value = jnp.concatenate([ref[h], jnp.zeros((24, 32), jnp.float32)], axis=1)
+            value = jnp.where(live, value, 0.0)
+            last = value[16:24]
+            stage[h, 16 * side:16 * side + 8] = jnp.where(lane8 < 96, value[0:8], pltpu.roll(last, 96, 1))
+            stage[h, 16 * side + 8:16 * side + 16] = jnp.where(lane8 < 96, value[8:16], pltpu.roll(last, 64, 1))
+            tail = pltpu.roll(last, 64, 1)
+            tails.append(jnp.where(lane8 < 32, tail, pltpu.roll(pltpu.roll(tail, 32, 1), 4, 0)))
+        stage[h, 32:36] = jnp.where(lane8 < 64, tails[0], pltpu.roll(tails[1], 64, 1))[0:4]
+    pl.semaphore_wait(barrier, len(callers))
 
     slot1 = (rank % 4) * 2 + core
-    sends1 = []
     for step in range(8):
         h = (owner + step) % 8
         to = (2 * (4 * h + band) + rank // 4, pan, rep)
-        sends1.append((stage.at[h], held.at[slot1], send1.at[step], recv1.at[slot1], to))
+        sends1.append((stage.at[h], held_packed.at[slot1], send1.at[step], recv1.at[slot1], to))
         start(*sends1[-1])
     for i in range(8):
-        arrived(held.at[i], recv1.at[i])
-
-    sends2 = []
+        arrived(held_packed.at[i], recv1.at[i])
+        four = jnp.concatenate([held_packed[i, 32:36], jnp.zeros((4, 128), jnp.float32)], axis=0)
+        for side in range(2):
+            one, two = held_packed[i, 16 * side:16 * side + 8], held_packed[i, 16 * side + 8:16 * side + 16]
+            tail = pltpu.roll(four, 64, 1) if side else four
+            row8 = lax.broadcasted_iota(jnp.int32, (8, 128), 0)
+            low = pltpu.roll(tail, 64, 1)
+            high = pltpu.roll(pltpu.roll(tail, 32, 1), 4, 0)
+            last = jnp.where(row8 < 4, low, high)
+            last = jnp.where(lane8 < 64, pltpu.roll(two, 64, 1), last)
+            last = jnp.where(lane8 < 32, pltpu.roll(one, 32, 1), last)
+            for start_row, value in ((0, one), (8, two), (16, last)):
+                held[i, 24 * side + start_row:24 * side + start_row + 8] = jnp.where(lane8 < 96, value, 0.0)
+
     for step in range(1, 4):
         y = (rep + step) % 4
         sends2.append((held.at[:, 0:24], amp_all.at[rep], send_a.at[step], recv_a.at[rep], (wide, pan, y)))
         remote(*sends2[-1]).start()
-    sends2b = []
     for step in range(4):
         to = (2 * (4 * owner + (layer + step) % 4) + core, pan, layer)
         sends2b.append((held.at[:, 24:48], int_all.at[core, rep], send_b.at[step], recv_b.at[rep], to))
         start(*sends2b[-1])
     own_amp = pltpu.make_async_copy(held.at[:, 0:24], amp_all.at[rep], send_a.at[0])
     own_amp.start()
-    sends2c = []
     for y in range(4):
         arrived(int_all.at[core, y], recv_b.at[y])
         sends2c.append((int_all.at[core, y], int_all.at[core, y], send_c.at[y], recv_c.at[y], (2 * z + 1 - core, pan, rep)))
@@ -100,7 +147,6 @@
                 (((1,), (1,)), ((), ())), precision=lax.Precision.HIGHEST, preferred_element_type=jnp.float32,
             )
         part[:, 192 * side:192 * (side + 1)] = total
-    sends3 = []
     for step in range(1, 4):
         x = (pan + step) % 4
         rows = part.at[pl.ds(pl.multiple_of(48 * x, 8), 48)]
@@ -112,31 +158,33 @@
         arrived(parts.at[x], recv3.at[x])
     cycle = parts[0] + parts[1] + parts[2] + parts[3]
 
-    flipped = jnp.concatenate([cycle, jnp.zeros((80, 384), jnp.float32)], axis=0).T
-    block_out[...] = flipped.reshape(8, 48, 128)
+    flipped = jnp.concatenate([cycle, jnp.zeros((80, 384), jnp.float32)], axis=0).T.reshape(8, 2, 24, 128)
+    right = pltpu.roll(flipped[:, 1].reshape(192, 128), 48, 1)
+    block_out[...] = flipped[:, 0] + right.reshape(8, 24, 128)
     mine = 4 * core + pan
-    sends4 = []
     for step in range(8):
         b = (mine + step) % 8
         to = (2 * (4 * owner + rep) + b // 4, b % 4, layer)
         sends4.append((block_out.at[b], block_in.at[mine], send4.at[step], recv4.at[mine], to))
         start(*sends4[-1])
-    mirror = jnp.zeros((48, 384), jnp.float32)
+    top, bottom = jnp.zeros((24, 384), jnp.float32), jnp.zeros((24, 384), jnp.float32)
+    wide_lane = lax.broadcasted_iota(jnp.int32, (24, 384), 1)
     for b in range(8):
         arrived(block_in.at[b], recv4.at[b])
-        widened = jnp.concatenate([block_in[b], jnp.zeros((48, 256), jnp.float32)], axis=1)
-        mirror = mirror + (pltpu.roll(widened, 48 * b, 1) if b else widened)
-    rows_out[...] = cycle + mirror
+        both = jnp.concatenate([block_in[b], jnp.zeros((24, 256), jnp.float32)], axis=1)
+        above = jnp.where(wide_lane < 48, both, 0.0)
+        top = top + (pltpu.roll(above, 48 * b, 1) if b else above)
+        below = both - above
+        bottom = bottom + (pltpu.roll(below, (48 * b + 336) % 384, 1) if b != 1 else below)
+    rows_out[0:24] = cycle[0:24] + top
+    rows_out[24:48] = cycle[24:48] + bottom
 
     columns = pl.ds(pl.multiple_of(384 * rep, 128), 384)
-    sends5 = []
     for c in range(2):
-        to = (2 * (8 * layer + 4 * core + pan) + c, (owner + layer) % 4, rep)
+        to = (2 * (8 * layer + 4 * core + pan) + c, (owner + pan) % 4, rep)
         sends5.append((rows_out.at[24 * c:24 * (c + 1)], out_ref.at[owner, :, columns], send5.at[c], recv5.at[owner // 4], to))
         start(*sends5[-1])
 
-    first = (pan + 4 - band) % 4
-    sends6 = []
     arrived(out_ref.at[first, :, columns], recv5.at[0])
     for step in range(1, 4):
         to = (wide, pan, (rep + step) % 4)
@@ -152,7 +200,6 @@
     for step in range(1, 4):
         y = (rep + step) % 4
         arrived(out_ref.at[first, :, pl.ds(pl.multiple_of(384 * y, 128), 384)], recv6.at[0, y])
-    sends7 = []
     for step in range(1, 4):
         to = (wide, (pan + step) % 4, rep)
         here = out_ref.at[first]
@@ -160,7 +207,7 @@
         remote(*sends7[-1]).start()
     for step in range(1, 4):
         x = (pan + step) % 4
-        arrived(out_ref.at[(x + 4 - band) % 4 + 4, :, columns], recv6.at[1, x])
+        arrived(out_ref.at[(x + 4 - z % 4) % 4 + 4, :, columns], recv6.at[1, x])
     for step in range(1, 4):
         to = (wide, pan, (rep + step) % 4)
         here = out_ref.at[4:8, :, columns]
@@ -168,41 +215,42 @@
         remote(*sends7[-1]).start()
     for step in range(1, 4):
         x = (pan + step) % 4
-        arrived(out_ref.at[(x + 4 - band) % 4], recv7.at[0, x])
+        arrived(out_ref.at[(x + 4 - z % 4) % 4], recv7.at[0, x])
     for step in range(1, 4):
         y = (rep + step) % 4
         arrived(out_ref.at[4:8, :, pl.ds(pl.multiple_of(384 * y, 128), 384)], recv7.at[1, y])
 
-    for args in sends1 + sends2b + sends4 + sends5:
-        finish_send(*args)
-    for args in sends2 + sends2c + sends3 + sends6 + sends7:
-        remote(*args).wait_send()
+    drain()
 
 
 def shards(amplitudes, integrals, pair_energies, block_sizes):
     vmem = pl.BlockSpec(memory_space=pltpu.VMEM)
+    hbm = pl.BlockSpec(memory_space=pl.ANY)
     dma = pltpu.SemaphoreType.DMA
     residual = pl.pallas_call(
         cycle_kernel,
         out_shape=jax.ShapeDtypeStruct((8, 24, 1536), jnp.float32),
-        in_specs=[pl.BlockSpec(memory_space=pltpu.SMEM), vmem, vmem],
+        in_specs=[pl.BlockSpec(memory_space=pltpu.SMEM), hbm, hbm],
         out_specs=vmem,
         scratch_shapes=[
-            pltpu.VMEM((8, 48, 128), jnp.float32),
+            pltpu.VMEM((8, 24, 96), jnp.float32),
+            pltpu.VMEM((8, 24, 96), jnp.float32),
+            pltpu.VMEM((8, 36, 128), jnp.float32),
+            pltpu.VMEM((8, 36, 128), jnp.float32),
             pltpu.VMEM((8, 48, 128), jnp.float32),
             pltpu.VMEM((4, 8, 24, 128), jnp.float32),
             pltpu.VMEM((2, 4, 8, 24, 128), jnp.float32),
             pltpu.VMEM((192, 384), jnp.float32),
             pltpu.VMEM((4, 48, 384), jnp.float32),
-            pltpu.VMEM((8, 48, 128), jnp.float32),
-            pltpu.VMEM((8, 48, 128), jnp.float32),
+            pltpu.VMEM((8, 24, 128), jnp.float32),
+            pltpu.VMEM((8, 24, 128), jnp.float32),
             pltpu.VMEM((48, 384), jnp.float32),
-            dma((8,)), dma((8,)),
+            dma((2,)), dma((8,)), dma((8,)),
             dma((4,)), dma((4,)), dma((4,)), dma((4,)), dma((4,)), dma((4,)),
             dma((4,)), dma((4,)), dma((8,)), dma((8,)), dma((2,)), dma((2,)),
             dma((2, 4)), dma((2, 4)), dma((2, 4)), dma((2, 4)),
         ],
-        compiler_params=pltpu.CompilerParams(has_side_effects=True, vmem_limit_bytes=24 * 1024 * 1024),
+        compiler_params=pltpu.CompilerParams(collective_id=0, has_side_effects=True, vmem_limit_bytes=24 * 1024 * 1024),
         cost_estimate=pl.CostEstimate(flops=60_000_000, bytes_accessed=2_000_000, transcendentals=0),
     )(block_sizes, amplitudes, jnp.swapaxes(integrals, 1, 2))
     row_start = lax.axis_index("wide") * 24

time: 132 us -> 114 us (0.86)
  the two profiles are of different devices: /device:TPU:1 before, /device:TPU:33 now
where the time goes in v2:
time: 114 us; the launch traced here: 113 us
  Pallas kernels  108 us (95%)
  local copies, waits for them, and re-layouts  3.53 us (3%)
  other arithmetic  1.24 us (1%)
    pallas_call x1, Pallas kernels, shards(): pl.pallas_call(cycle_kernel, out_shape=jax.ShapeDtypeStruct((8, 24, 1536)...  108 us
    unnamed x9, local copies, waits for them, and re-layouts  3.45 us

profile of v2, /device:TPU:33, one launch (start us, length us, event | category | flops | bytes accessed | tf_op | source)
XLA Modules:
  0.0 113.4 jit_solution(16605647450793603401)
XLA Ops:
  0.6 0.0 copy-start
  0.6 0.9 copy-done
  1.5 0.0 copy-start.1
  1.5 0.9 copy-done.1
  2.4 0.0 copy-start.2
  2.4 0.7 copy-done.2
  3.1 0.0 copy-start.3
  3.1 107.9 %shard_map.59 = f32[8,24,1536]{2,1,0:T(8,128)S(1)} custom-call(s32[8]{0:T(128)S(1)} %copy-done.2, f32[8,24,96]{2,1,0:T(8,128)S(1)} %copy-done, f32[8,24,96]{2,1,0:T(8,128)S(1)} %bitcast.1), custom_call_target="tpu_custom_call" | custom-call | flops 60000000 | bytes 2000000 | tf_op jit(solution)/shard_map/pallas_call | solution.py:230
  111.0 0.0 copy-done.3
  111.0 0.1 constant_dynamic-slice_fusion
  111.1 1.2 %add_divide_fusion = f32[8,24,1536]{2,1,0:T(8,128)} fusion(f32[8,24,1536]{2,1,0:T(8,128)S(1)} %shard_map.59, f32[8,1536]{1,0:T(8,128)S(1)} %copy-done.3, f32[8,24]{1,0:T(8,128)S(1)} %constant_dynamic-slice_fusion), kind=kLoop, calls=%fused_computation | loop fusion | flops 884736 | bytes 2409216 | tf_op jit(solution)/shard_map/div | solution.py:258
  112.4 1.0 copy.7
Async XLA Ops:
  0.6 0.9 copy-start
  1.5 0.9 copy-start.1
  2.4 0.7 copy-start.2
  3.1 108.0 %copy-start.3 = (f32[8,1536]{1,0:T(8,128)S(1)}, f32[8,1536]{1,0:T(8,128)}, u32[]{:S(2)}) copy-start(f32[8,1536]{1,0:T(8,128)} %param.6) | copy-start | bytes 147460

commit v3 on v2

v3 whole, which is shorter than its diff:
```python
import jax
import jax.numpy as jnp
from jax import lax
from jax.experimental import pallas as pl
from jax.experimental.pallas import tpu as pltpu
from jax.sharding import PartitionSpec as P

MESH = pl.DeviceIdType.MESH


def cycle_kernel(
    sizes_ref, amp_hbm, int_hbm, out_ref,
    amp_ref, int_ref, stage, amp_packed, int_packed, amp_all, int_all, part, parts, block_out, block_in, rows_out,
    load, send1, recv1, send_a, recv_a, send_b, recv_b, send_c, recv_c,
    send3, recv3, send4, recv4, send5, recv5, send6, recv6, send7, recv7, send8, recv8,
):
    wide, pan, rep = lax.axis_index("wide"), lax.axis_index("pan"), lax.axis_index("rep")
    z, core = wide // 2, wide % 2
    owner, layer = z // 4, z % 4
    band, rank = z // 8, z % 8

    def device(w, x, y):
        return {"wide": w, "pan": x, "rep": y}

    def remote(src, dst, ssem, rsem, to):
        return pltpu.make_async_remote_copy(
            src_ref=src, dst_ref=dst, send_sem=ssem, recv_sem=rsem,
            device_id=device(*to), device_id_type=MESH,
        )

    def is_me(to):
        return (to[0] == wide) & (to[1] == pan) & (to[2] == rep)

    def start(src, dst, ssem, rsem, to):
        me = is_me(to)

        @pl.when(me)
        def _():
            pltpu.make_async_copy(src, dst, rsem).start()

        @pl.when(jnp.logical_not(me))
        def _():
            remote(src, dst, ssem, rsem, to).start()

    def finish_send(src, dst, ssem, rsem, to):
        @pl.when(jnp.logical_not(is_me(to)))
        def _():
            remote(src, dst, ssem, rsem, to).wait_send()

    def arrived(dst, rsem):
        pltpu.make_async_copy(dst, dst, rsem).wait()

    sent, sent_or_kept = [], []

    def send(*args):
        sent.append(args)
        remote(*args).start()

    def send_or_keep(*args):
        sent_or_kept.append(args)
        start(*args)

    loads = [
        pltpu.make_async_copy(amp_hbm, amp_ref, load.at[0]),
        pltpu.make_async_copy(int_hbm, int_ref, load.at[1]),
    ]
    for copy in loads:
        copy.start()

    first = (pan + 4 - z % 4) % 4
    callers = [(2 * (8 * layer + 4 * core + i // 2) + i % 2, pan, rep) for i in range(8)]
    callers += [(2 * (8 * rep + 4 * core + i // 2) + i % 2, pan, layer) for i in range(8)]
    callers += [(wide, pan, (rep + step) % 4) for step in range(1, 4)]
    callers += [(wide, (pan + step) % 4, rep) for step in range(1, 4)]
    callers += [(2 * z + 1 - core, pan, rep)]
    callers += [(2 * (4 * owner + (layer + step) % 4) + core, pan, rep) for step in range(1, 4)]
    callers += [(2 * (4 * owner + rep) + b // 4, b % 4, layer) for b in range(8)]
    callers += [(2 * (4 * (first + 4 * i) + band) + rank // 4, z % 4, rep) for i in range(2)]
    barrier = pltpu.get_barrier_semaphore()
    for to in callers:
        pl.semaphore_signal(barrier, inc=1, device_id=device(*to), device_id_type=MESH)

    row_at = wide * 24 + lax.broadcasted_iota(jnp.int32, (24, 128), 0)
    lane = lax.broadcasted_iota(jnp.int32, (24, 128), 1)
    sum_at = (pan * 4 + rep) * 96 + lane
    lane8 = lane[0:8]
    for copy in loads:
        copy.wait()
    for h in range(8):
        live = (row_at < sizes_ref[h]) & (sum_at < sizes_ref[h]) & (lane < 96)
        for side, ref in enumerate((amp_ref, int_ref)):
            value = jnp.concatenate([ref[h], jnp.zeros((24, 32), jnp.float32)], axis=1)
            value = jnp.where(live, value, 0.0)
            last = value[16:24]
            stage[side, h, 0:8] = jnp.where(lane8 < 96, value[0:8], pltpu.roll(last, 96, 1))
            stage[side, h, 8:16] = jnp.where(lane8 < 96, value[8:16], pltpu.roll(last, 64, 1))
            pairs = pltpu.roll(last, 64, 1)
            pairs = jnp.where(lane8 < 32, pairs, pltpu.roll(pltpu.roll(last, 96, 1), 6, 0))
            pairs = jnp.where(lane8 < 64, pairs, pltpu.roll(last, 4, 0))
            pairs = jnp.where(lane8 < 96, pairs, pltpu.roll(pltpu.roll(last, 32, 1), 2, 0))
            stage[side, h, 16:18] = pairs[0:2]
    pl.semaphore_wait(barrier, len(callers))

    slot1 = (rank % 4) * 2 + core
    for step in (4, 3, 5, 2, 6, 1, 7, 0):
        h = (owner + step) % 8
        to = (2 * (4 * h + band) + rank // 4, pan, rep)
        send_or_keep(stage.at[0, h], amp_packed.at[rep, slot1], send1.at[0, step], recv1.at[0, slot1], to)
        to = (2 * (4 * h + rep) + rank // 4, pan, band)
        send_or_keep(stage.at[1, h], int_packed.at[rank // 4, rep, slot1], send1.at[1, step], recv1.at[1, slot1], to)

    sibling = (2 * z + 1 - core, pan, rep)
    for pair in range(4):
        two = slice(2 * pair, 2 * pair + 2)
        for i in (2 * pair, 2 * pair + 1):
            arrived(amp_packed.at[rep, i], recv1.at[0, i])
        here = amp_packed.at[rep, two]
        for step in range(1, 4):
            send(here, here, send_a.at[pair, step], recv_a.at[pair, rep], (wide, pan, (rep + step) % 4))
        for i in (2 * pair, 2 * pair + 1):
            arrived(int_packed.at[core, layer, i], recv1.at[1, i])
        here = int_packed.at[core, layer, two]
        for step in range(1, 4):
            to = (2 * (4 * owner + (layer + step) % 4) + core, pan, rep)
            send(here, here, send_b.at[pair, step], recv_b.at[pair, layer], to)
        send(here, here, send_c.at[pair, 0], recv_c.at[pair, layer], sibling)

    def unpack(packed, whole, index, mask):
        for i in range(8):
            one, two = packed[index + (i, slice(0, 8))], packed[index + (i, slice(8, 16))]
            tail = jnp.concatenate([packed[index + (i, slice(16, 18))], jnp.zeros((6, 128), jnp.float32)], axis=0)
            last = pltpu.roll(tail, 64, 1) + pltpu.roll(pltpu.roll(tail, 32, 1), 2, 0)
            last = last + pltpu.roll(tail, 4, 0) + pltpu.roll(pltpu.roll(tail, 96, 1), 6, 0)
            last = jnp.where(lane8 < 64, pltpu.roll(two, 64, 1), last)
            last = jnp.where(lane8 < 32, pltpu.roll(one, 32, 1), last)
            for row, value in ((0, one), (8, two), (16, last)):
                whole[index + (slice(24 * i + row, 24 * i + row + 8),)] = jnp.where(lane8 < 96, value, 0.0) if mask else value

    unpack(amp_packed, amp_all, (rep,), True)
    unpack(int_packed, int_all, (core, layer), False)
    for step in (1, 3, 2):
        y, l = (rep + step) % 4, (layer + step) % 4
        for pair in range(4):
            two = slice(2 * pair, 2 * pair + 2)
            arrived(int_packed.at[core, l, two], recv_b.at[pair, l])
            here = int_packed.at[core, l, two]
            send(here, here, send_c.at[pair, step], recv_c.at[pair, l], sibling)
        unpack(int_packed, int_all, (core, l), False)
        for pair in range(4):
            arrived(amp_packed.at[y, 2 * pair:2 * pair + 2], recv_a.at[pair, y])
        unpack(amp_packed, amp_all, (y,), True)
    for step in (0, 1, 3, 2):
        l = (layer + step) % 4
        for pair in range(4):
            arrived(int_packed.at[1 - core, l, 2 * pair:2 * pair + 2], recv_c.at[pair, l])
        unpack(int_packed, int_all, (1 - core, l), False)

    for side in range(2):
        total = jnp.zeros((192, 192), jnp.float32)
        for y in range(4):
            total = total + lax.dot_general(
                amp_all[y], int_all[side, y],
                (((1,), (1,)), ((), ())), precision=lax.Precision.HIGHEST, preferred_element_type=jnp.float32,
            )
        part[:, 192 * side:192 * (side + 1)] = total
    for step in range(1, 4):
        x = (pan + step) % 4
        rows = part.at[pl.ds(pl.multiple_of(48 * x, 8), 48)]
        send(rows, parts.at[pan], send3.at[step], recv3.at[pan], (wide, x, rep))
    parts[pan] = part[pl.ds(pl.multiple_of(48 * pan, 8), 48)]
    for step in range(1, 4):
        x = (pan + step) % 4
        arrived(parts.at[x], recv3.at[x])
    cycle = parts[0] + parts[1] + parts[2] + parts[3]

    flipped = jnp.concatenate([cycle, jnp.zeros((80, 384), jnp.float32)], axis=0).T.reshape(8, 2, 24, 128)
    right = pltpu.roll(flipped[:, 1].reshape(192, 128), 48, 1)
    block_out[...] = flipped[:, 0] + right.reshape(8, 24, 128)
    mine = 4 * core + pan
    for step in range(8):
        b = (mine + step) % 8
        to = (2 * (4 * owner + rep) + b // 4, b % 4, layer)
        send_or_keep(block_out.at[b], block_in.at[mine], send4.at[step], recv4.at[mine], to)
    top, bottom = jnp.zeros((24, 384), jnp.float32), jnp.zeros((24, 384), jnp.float32)
    wide_lane = lax.broadcasted_iota(jnp.int32, (24, 384), 1)
    for b in range(8):
        arrived(block_in.at[b], recv4.at[b])
        both = jnp.concatenate([block_in[b], jnp.zeros((24, 256), jnp.float32)], axis=1)
        above = jnp.where(wide_lane < 48, both, 0.0)
        top = top + (pltpu.roll(above, 48 * b, 1) if b else above)
        below = both - above
        bottom = bottom + (pltpu.roll(below, (48 * b + 336) % 384, 1) if b != 1 else below)
    rows_out[0:24] = cycle[0:24] + top
    rows_out[24:48] = cycle[24:48] + bottom

    columns = pl.ds(pl.multiple_of(384 * rep, 128), 384)
    for c in range(2):
        to = (2 * (8 * layer + 4 * core + pan) + c, (owner + pan) % 4, rep)
        send_or_keep(rows_out.at[24 * c:24 * (c + 1)], out_ref.at[owner, :, columns], send5.at[c], recv5.at[owner // 4], to)

    def place(half, i, j):
        x, y = (pan + j, rep + i) if half == 0 else (pan + i, rep + j)
        return x % 4, y % 4

    def rows(half, i, j):
        x, y = place(half, i, j)
        return out_ref.at[(x + 4 - z % 4) % 4 + 4 * half, :, pl.ds(pl.multiple_of(384 * y, 128), 384)]

    def to_neighbours(half, i):
        here = rows(half, i, 0)
        for way in (1, 3):
            send(here, here, send7.at[half, way // 2, i], recv7.at[half, way // 2, i], (wide,) + place(half, 0, way))

    for half in range(2):
        here = rows(half, 0, 0)
        arrived(here, recv5.at[half])
        for i in (1, 3, 2):
            send(here, here, send6.at[half, i], recv6.at[half, 4 - i], (wide,) + place(half, i, 0))
        to_neighbours(half, 0)
    for i in (1, 3, 2):
        for half in range(2):
            arrived(rows(half, i, 0), recv6.at[half, i])
            to_neighbours(half, i)
    for i in (0, 1, 3, 2):
        for half in range(2):
            arrived(rows(half, i, 3), recv7.at[half, 0, i])
            arrived(rows(half, i, 1), recv7.at[half, 1, i])
            come, go = (1, 3) if i < 2 else (3, 1)
            here = rows(half, i, come)
            send(here, here, send8.at[half, i], recv8.at[half, i], (wide,) + place(half, 0, go))
    for i in (0, 1, 3, 2):
        for half in range(2):
            arrived(rows(half, i, 2), recv8.at[half, i])

    for args in sent:
        remote(*args).wait_send()
    for args in sent_or_kept:
        finish_send(*args)


def shards(amplitudes, integrals, pair_energies, block_sizes):
    vmem = pl.BlockSpec(memory_space=pltpu.VMEM)
    hbm = pl.BlockSpec(memory_space=pltpu.HBM)
    dma = pltpu.SemaphoreType.DMA
    residual = pl.pallas_call(
        cycle_kernel,
        out_shape=jax.ShapeDtypeStruct((8, 24, 1536), jnp.float32),
        in_specs=[pl.BlockSpec(memory_space=pltpu.SMEM), hbm, hbm],
        out_specs=vmem,
        scratch_shapes=[
            pltpu.VMEM((8, 24, 96), jnp.float32),
            pltpu.VMEM((8, 24, 96), jnp.float32),
            pltpu.VMEM((2, 8, 18, 128), jnp.float32),
            pltpu.VMEM((4, 8, 18, 128), jnp.float32),
            pltpu.VMEM((2, 4, 8, 18, 128), jnp.float32),
            pltpu.VMEM((4, 192, 128), jnp.float32),
            pltpu.VMEM((2, 4, 192, 128), jnp.float32),
            pltpu.VMEM((192, 384), jnp.float32),
            pltpu.VMEM((4, 48, 384), jnp.float32),
            pltpu.VMEM((8, 24, 128), jnp.float32),
            pltpu.VMEM((8, 24, 128), jnp.float32),
            pltpu.VMEM((48, 384), jnp.float32),
            dma((2,)), dma((2, 8)), dma((2, 8)),
            dma((4, 4)), dma((4, 4)), dma((4, 4)), dma((4, 4)), dma((4, 4)), dma((4, 4)),
            dma((4,)), dma((4,)), dma((8,)), dma((8,)), dma((2,)), dma((2,)),
            dma((2, 4)), dma((2, 4)), dma((2, 2, 4)), dma((2, 2, 4)), dma((2, 4)), dma((2, 4)),
        ],
        compiler_params=pltpu.CompilerParams(collective_id=0, has_side_effects=True, vmem_limit_bytes=24 * 1024 * 1024),
        cost_estimate=pl.CostEstimate(flops=60_000_000, bytes_accessed=2_000_000, transcendentals=0),
    )(block_sizes, amplitudes, jnp.swapaxes(integrals, 1, 2))
    row_start = lax.axis_index("wide") * 24
    energy_rows = lax.dynamic_slice_in_dim(pair_energies, row_start, 24, 1)
    update = -residual / (energy_rows[:, :, None] + pair_energies[:, None, :])
    return (residual, update)


def solution(mesh):
    in_specs = (P(None, "wide", ("pan", "rep")), P(None, ("pan", "rep"), "wide"), P(), P())
    out_specs = (P(None, "wide", None), P(None, "wide", None))
    return jax.shard_map(shards, mesh=mesh, in_specs=in_specs, out_specs=out_specs, check_vma=False)
```

time: 114 us -> 108 us (0.947)
  the two profiles are of different devices: /device:TPU:33 before, /device:TPU:1 now
where the time goes in v3:
time: 108 us; the launch traced here: 106 us
  Pallas kernels  100 us (93%)
  local copies, waits for them, and re-layouts  3.53 us (3%)
  other arithmetic  1.24 us (1%)
    pallas_call x1, Pallas kernels, shards(): pl.pallas_call(cycle_kernel, out_shape=jax.ShapeDtypeStruct((8, 24, 1536)...  100 us
    unnamed x9, local copies, waits for them, and re-layouts  3.45 us

profile of v3, /device:TPU:1, one launch (start us, length us, event | category | flops | bytes accessed | tf_op | source)
XLA Modules:
  0.0 105.9 jit_solution(5045237911337235744)
XLA Ops:
  0.6 0.0 copy-start
  0.6 0.9 copy-done
  1.5 0.0 copy-start.1
  1.5 0.9 copy-done.1
  2.4 0.0 copy-start.2
  2.4 0.7 copy-done.2
  3.1 0.0 copy-start.3
  3.1 100.5 %shard_map.59 = f32[8,24,1536]{2,1,0:T(8,128)S(1)} custom-call(s32[8]{0:T(128)S(1)} %copy-done.2, f32[8,24,96]{2,1,0:T(8,128)S(1)} %copy-done, f32[8,24,96]{2,1,0:T(8,128)S(1)} %bitcast.1), custom_call_target="tpu_custom_call" | custom-call | flops 60000000 | bytes 2000000 | tf_op jit(solution)/shard_map/pallas_call | solution.py:245
  103.6 0.0 copy-done.3
  103.6 0.1 constant_dynamic-slice_fusion
  103.7 1.2 %add_divide_fusion = f32[8,24,1536]{2,1,0:T(8,128)} fusion(f32[8,24,1536]{2,1,0:T(8,128)S(1)} %shard_map.59, f32[8,1536]{1,0:T(8,128)S(1)} %copy-done.3, f32[8,24]{1,0:T(8,128)S(1)} %constant_dynamic-slice_fusion), kind=kLoop, calls=%fused_computation | loop fusion | flops 884736 | bytes 2409216 | tf_op jit(solution)/shard_map/div | solution.py:273
  104.9 1.0 copy.7
Async XLA Ops:
  0.6 0.9 copy-start
  1.5 0.9 copy-start.1
  2.4 0.7 copy-start.2
  3.1 100.5 %copy-start.3 = (f32[8,1536]{1,0:T(8,128)S(1)}, f32[8,1536]{1,0:T(8,128)}, u32[]{:S(2)}) copy-start(f32[8,1536]{1,0:T(8,128)} %param.6) | copy-start | bytes 147460

commit v4 on v3

--- a/solution.py
+++ b/solution.py
@@ -9,8 +9,8 @@
 
 
 def cycle_kernel(
-    sizes_ref, amp_hbm, int_hbm, out_ref,
-    amp_ref, int_ref, stage, amp_packed, int_packed, amp_all, int_all, part, parts, block_out, block_in, rows_out,
+    sizes_hbm, amp_hbm, int_hbm, out_ref,
+    sizes_ref, amp_ref, int_ref, stage, amp_packed, int_packed, amp_all, int_all, part, parts, block_out, block_in, rows_out,
     load, send1, recv1, send_a, recv_a, send_b, recv_b, send_c, recv_c,
     send3, recv3, send4, recv4, send5, recv5, send6, recv6, send7, recv7, send8, recv8,
 ):
@@ -63,11 +63,16 @@
     loads = [
         pltpu.make_async_copy(amp_hbm, amp_ref, load.at[0]),
         pltpu.make_async_copy(int_hbm, int_ref, load.at[1]),
+        pltpu.make_async_copy(sizes_hbm, sizes_ref, load.at[2]),
     ]
     for copy in loads:
         copy.start()
 
-    first = (pan + 4 - z % 4) % 4
+    def block_at(x, at, far):
+        one = (x + 4 - at % 4) % 4
+        off = (4 * one + 2 + 32 - at) % 32
+        return (one + 4 * (((off + 7) % 32) // 16) + 4 * far) % 8
+
     callers = [(2 * (8 * layer + 4 * core + i // 2) + i % 2, pan, rep) for i in range(8)]
     callers += [(2 * (8 * rep + 4 * core + i // 2) + i % 2, pan, layer) for i in range(8)]
     callers += [(wide, pan, (rep + step) % 4) for step in range(1, 4)]
@@ -75,7 +80,7 @@
     callers += [(2 * z + 1 - core, pan, rep)]
     callers += [(2 * (4 * owner + (layer + step) % 4) + core, pan, rep) for step in range(1, 4)]
     callers += [(2 * (4 * owner + rep) + b // 4, b % 4, layer) for b in range(8)]
-    callers += [(2 * (4 * (first + 4 * i) + band) + rank // 4, z % 4, rep) for i in range(2)]
+    callers += [(2 * (4 * block_at(pan, z, far) + band) + rank // 4, z % 4, rep) for far in range(2)]
     barrier = pltpu.get_barrier_semaphore()
     for to in callers:
         pl.semaphore_signal(barrier, inc=1, device_id=device(*to), device_id_type=MESH)
@@ -190,13 +195,16 @@
         top = top + (pltpu.roll(above, 48 * b, 1) if b else above)
         below = both - above
         bottom = bottom + (pltpu.roll(below, (48 * b + 336) % 384, 1) if b != 1 else below)
-    rows_out[0:24] = cycle[0:24] + top
-    rows_out[24:48] = cycle[24:48] + bottom
+    rows_out[0:24] = -(cycle[0:24] + top)
+    rows_out[24:48] = -(cycle[24:48] + bottom)
 
     columns = pl.ds(pl.multiple_of(384 * rep, 128), 384)
+    goal = 8 * layer + 4 * core + pan
+    column = (owner + pan) % 4
+    far = ((owner + 8 - block_at(column, goal, 0)) % 8) // 4
     for c in range(2):
-        to = (2 * (8 * layer + 4 * core + pan) + c, (owner + pan) % 4, rep)
-        send_or_keep(rows_out.at[24 * c:24 * (c + 1)], out_ref.at[owner, :, columns], send5.at[c], recv5.at[owner // 4], to)
+        to = (2 * goal + c, column, rep)
+        send_or_keep(rows_out.at[24 * c:24 * (c + 1)], out_ref.at[owner, :, columns], send5.at[c], recv5.at[far], to)
 
     def place(half, i, j):
         x, y = (pan + j, rep + i) if half == 0 else (pan + i, rep + j)
@@ -204,7 +212,7 @@
 
     def rows(half, i, j):
         x, y = place(half, i, j)
-        return out_ref.at[(x + 4 - z % 4) % 4 + 4 * half, :, pl.ds(pl.multiple_of(384 * y, 128), 384)]
+        return out_ref.at[block_at(x, z, half), :, pl.ds(pl.multiple_of(384 * y, 128), 384)]
 
     def to_neighbours(half, i):
         here = rows(half, i, 0)
@@ -217,19 +225,17 @@
         for i in (1, 3, 2):
             send(here, here, send6.at[half, i], recv6.at[half, 4 - i], (wide,) + place(half, i, 0))
         to_neighbours(half, 0)
-    for i in (1, 3, 2):
-        for half in range(2):
+        for i in (1, 3, 2):
             arrived(rows(half, i, 0), recv6.at[half, i])
             to_neighbours(half, i)
-    for i in (0, 1, 3, 2):
-        for half in range(2):
-            arrived(rows(half, i, 3), recv7.at[half, 0, i])
-            arrived(rows(half, i, 1), recv7.at[half, 1, i])
+        for i in (0, 1, 3, 2):
             come, go = (1, 3) if i < 2 else (3, 1)
             here = rows(half, i, come)
+            arrived(here, recv7.at[half, 1 if i < 2 else 0, i])
             send(here, here, send8.at[half, i], recv8.at[half, i], (wide,) + place(half, 0, go))
-    for i in (0, 1, 3, 2):
-        for half in range(2):
+    for half in range(2):
+        for i in range(4):
+            arrived(rows(half, i, 3 if i < 2 else 1), recv7.at[half, 0 if i < 2 else 1, i])
             arrived(rows(half, i, 2), recv8.at[half, i])
 
     for args in sent:
@@ -242,12 +248,13 @@
     vmem = pl.BlockSpec(memory_space=pltpu.VMEM)
     hbm = pl.BlockSpec(memory_space=pltpu.HBM)
     dma = pltpu.SemaphoreType.DMA
-    residual = pl.pallas_call(
+    negated = pl.pallas_call(
         cycle_kernel,
         out_shape=jax.ShapeDtypeStruct((8, 24, 1536), jnp.float32),
-        in_specs=[pl.BlockSpec(memory_space=pltpu.SMEM), hbm, hbm],
+        in_specs=[hbm, hbm, hbm],
         out_specs=vmem,
         scratch_shapes=[
+            pltpu.SMEM((8,), jnp.int32),
             pltpu.VMEM((8, 24, 96), jnp.float32),
             pltpu.VMEM((8, 24, 96), jnp.float32),
             pltpu.VMEM((2, 8, 18, 128), jnp.float32),
@@ -260,18 +267,18 @@
             pltpu.VMEM((8, 24, 128), jnp.float32),
             pltpu.VMEM((8, 24, 128), jnp.float32),
             pltpu.VMEM((48, 384), jnp.float32),
-            dma((2,)), dma((2, 8)), dma((2, 8)),
+            dma((3,)), dma((2, 8)), dma((2, 8)),
             dma((4, 4)), dma((4, 4)), dma((4, 4)), dma((4, 4)), dma((4, 4)), dma((4, 4)),
             dma((4,)), dma((4,)), dma((8,)), dma((8,)), dma((2,)), dma((2,)),
             dma((2, 4)), dma((2, 4)), dma((2, 2, 4)), dma((2, 2, 4)), dma((2, 4)), dma((2, 4)),
         ],
         compiler_params=pltpu.CompilerParams(collective_id=0, has_side_effects=True, vmem_limit_bytes=24 * 1024 * 1024),
         cost_estimate=pl.CostEstimate(flops=60_000_000, bytes_accessed=2_000_000, transcendentals=0),
-    )(block_sizes, amplitudes, jnp.swapaxes(integrals, 1, 2))
+    )(*(pltpu.with_memory_space_constraint(operand, pltpu.HBM) for operand in (block_sizes, amplitudes, jnp.swapaxes(integrals, 1, 2))))
     row_start = lax.axis_index("wide") * 24
     energy_rows = lax.dynamic_slice_in_dim(pair_energies, row_start, 24, 1)
-    update = -residual / (energy_rows[:, :, None] + pair_energies[:, None, :])
-    return (residual, update)
+    update = negated / (energy_rows[:, :, None] + pair_energies[:, None, :])
+    return (-negated, update)
 
 
 def solution(mesh):

time: 108 us -> 109 us (level)
  the two profiles are of different devices: /device:TPU:1 before, /device:TPU:64 now
where the time goes in v4:
time: 109 us
  Pallas kernels  105 us (96%)
  other arithmetic  1.61 us (1%)
    pallas_call x1, Pallas kernels, shards(): pl.pallas_call(cycle_kernel, out_shape=jax.ShapeDtypeStruct((8, 24, 1536)...  105 us

profile of v4, /device:TPU:64, one launch (start us, length us, event | category | flops | bytes accessed | tf_op | source)
XLA Modules:
  0.0 108.6 jit_solution(11492945464626248538)
XLA Ops:
  0.6 0.0 copy-start
  0.6 0.8 constant_dynamic-slice_fusion
  1.5 105.5 %shard_map.59 = f32[8,24,1536]{2,1,0:T(8,128)S(1)} custom-call(s32[8]{0:T(128)} %sizes_hbm.1, f32[8,24,96]{2,1,0:T(8,128)} %amp_hbm.1, f32[8,24,96]{2,1,0:T(8,128)} %bitcast.1), custom_call_target="tpu_custom_call" | custom-call | flops 60000000 | bytes 2000000 | tf_op jit(solution)/shard_map/pallas_call | solution.py:251
  107.0 0.0 copy-done
  107.0 1.6 %add_divide_fusion = (f32[8,24,1536]{2,1,0:T(8,128)}, f32[8,24,1536]{2,1,0:T(8,128)}) fusion(f32[8,24,1536]{2,1,0:T(8,128)S(1)} %shard_map.59, f32[8,1536]{1,0:T(8,128)S(1)} %copy-done, f32[8,24]{1,0:T(8,128)S(1)} %constant_dynamic-slice_fusion), kind=kLoop, calls=%fused_computation | loop fusion | flops 884736 | bytes 3588864 | tf_op jit(solution)/shard_map/div | solution.py:280
Async XLA Ops:
  0.6 106.3 %copy-start = (f32[8,1536]{1,0:T(8,128)S(1)}, f32[8,1536]{1,0:T(8,128)}, u32[]{:S(2)}) copy-start(f32[8,1536]{1,0:T(8,128)} %param.6) | copy-start | bytes 147460

commit v5 on v4

--- a/solution.py
+++ b/solution.py
@@ -89,6 +89,25 @@
     lane = lax.broadcasted_iota(jnp.int32, (24, 128), 1)
     sum_at = (pan * 4 + rep) * 96 + lane
     lane8 = lane[0:8]
+
+    def pack(value):
+        last = value[16:24]
+        pairs = jnp.where(lane8 < 32, pltpu.roll(last, 64, 1), pltpu.roll(pltpu.roll(last, 96, 1), 6, 0))
+        pairs = jnp.where(lane8 < 64, pairs, pltpu.roll(last, 4, 0))
+        pairs = jnp.where(lane8 < 96, pairs, pltpu.roll(pltpu.roll(last, 32, 1), 2, 0))
+        return (
+            jnp.where(lane8 < 96, value[0:8], pltpu.roll(last, 96, 1)),
+            jnp.where(lane8 < 96, value[8:16], pltpu.roll(last, 64, 1)),
+            pairs[0:2],
+        )
+
+    def unpack(one, two, tail):
+        tail = jnp.concatenate([tail, jnp.zeros((6, 128), jnp.float32)], axis=0)
+        last = pltpu.roll(tail, 64, 1) + pltpu.roll(pltpu.roll(tail, 32, 1), 2, 0)
+        last = last + pltpu.roll(tail, 4, 0) + pltpu.roll(pltpu.roll(tail, 96, 1), 6, 0)
+        last = jnp.where(lane8 < 64, pltpu.roll(two, 64, 1), last)
+        return one, two, jnp.where(lane8 < 32, pltpu.roll(one, 32, 1), last)
+
     for copy in loads:
         copy.wait()
     for h in range(8):
@@ -96,14 +115,8 @@
         for side, ref in enumerate((amp_ref, int_ref)):
             value = jnp.concatenate([ref[h], jnp.zeros((24, 32), jnp.float32)], axis=1)
             value = jnp.where(live, value, 0.0)
-            last = value[16:24]
-            stage[side, h, 0:8] = jnp.where(lane8 < 96, value[0:8], pltpu.roll(last, 96, 1))
-            stage[side, h, 8:16] = jnp.where(lane8 < 96, value[8:16], pltpu.roll(last, 64, 1))
-            pairs = pltpu.roll(last, 64, 1)
-            pairs = jnp.where(lane8 < 32, pairs, pltpu.roll(pltpu.roll(last, 96, 1), 6, 0))
-            pairs = jnp.where(lane8 < 64, pairs, pltpu.roll(last, 4, 0))
-            pairs = jnp.where(lane8 < 96, pairs, pltpu.roll(pltpu.roll(last, 32, 1), 2, 0))
-            stage[side, h, 16:18] = pairs[0:2]
+            for row, part_of in zip((0, 8, 16), pack(value)):
+                stage[side, h, row:row + part_of.shape[0]] = part_of
     pl.semaphore_wait(barrier, len(callers))
 
     slot1 = (rank % 4) * 2 + core
@@ -130,19 +143,14 @@
             send(here, here, send_b.at[pair, step], recv_b.at[pair, layer], to)
         send(here, here, send_c.at[pair, 0], recv_c.at[pair, layer], sibling)
 
-    def unpack(packed, whole, index, mask):
+    def spread(packed, whole, index, mask):
         for i in range(8):
-            one, two = packed[index + (i, slice(0, 8))], packed[index + (i, slice(8, 16))]
-            tail = jnp.concatenate([packed[index + (i, slice(16, 18))], jnp.zeros((6, 128), jnp.float32)], axis=0)
-            last = pltpu.roll(tail, 64, 1) + pltpu.roll(pltpu.roll(tail, 32, 1), 2, 0)
-            last = last + pltpu.roll(tail, 4, 0) + pltpu.roll(pltpu.roll(tail, 96, 1), 6, 0)
-            last = jnp.where(lane8 < 64, pltpu.roll(two, 64, 1), last)
-            last = jnp.where(lane8 < 32, pltpu.roll(one, 32, 1), last)
-            for row, value in ((0, one), (8, two), (16, last)):
+            values = unpack(*(packed[index + (i, slice(*rows))] for rows in ((0, 8), (8, 16), (16, 18))))
+            for row, value in zip((0, 8, 16), values):
                 whole[index + (slice(24 * i + row, 24 * i + row + 8),)] = jnp.where(lane8 < 96, value, 0.0) if mask else value
 
-    unpack(amp_packed, amp_all, (rep,), True)
-    unpack(int_packed, int_all, (core, layer), False)
+    spread(amp_packed, amp_all, (rep,), True)
+    spread(int_packed, int_all, (core, layer), False)
     for step in (1, 3, 2):
         y, l = (rep + step) % 4, (layer + step) % 4
         for pair in range(4):
@@ -150,15 +158,15 @@
             arrived(int_packed.at[core, l, two], recv_b.at[pair, l])
             here = int_packed.at[core, l, two]
             send(here, here, send_c.at[pair, step], recv_c.at[pair, l], sibling)
-        unpack(int_packed, int_all, (core, l), False)
+        spread(int_packed, int_all, (core, l), False)
         for pair in range(4):
             arrived(amp_packed.at[y, 2 * pair:2 * pair + 2], recv_a.at[pair, y])
-        unpack(amp_packed, amp_all, (y,), True)
+        spread(amp_packed, amp_all, (y,), True)
     for step in (0, 1, 3, 2):
         l = (layer + step) % 4
         for pair in range(4):
             arrived(int_packed.at[1 - core, l, 2 * pair:2 * pair + 2], recv_c.at[pair, l])
-        unpack(int_packed, int_all, (1 - core, l), False)
+        spread(int_packed, int_all, (1 - core, l), False)
 
     for side in range(2):
         total = jnp.zeros((192, 192), jnp.float32)
@@ -180,7 +188,10 @@
 
     flipped = jnp.concatenate([cycle, jnp.zeros((80, 384), jnp.float32)], axis=0).T.reshape(8, 2, 24, 128)
     right = pltpu.roll(flipped[:, 1].reshape(192, 128), 48, 1)
-    block_out[...] = flipped[:, 0] + right.reshape(8, 24, 128)
+    paired = flipped[:, 0] + right.reshape(8, 24, 128)
+    for b in range(8):
+        for row, part_of in zip((0, 8, 16), pack(paired[b])):
+            block_out[b, row:row + part_of.shape[0]] = part_of
     mine = 4 * core + pan
     for step in range(8):
         b = (mine + step) % 8
@@ -190,7 +201,8 @@
     wide_lane = lax.broadcasted_iota(jnp.int32, (24, 384), 1)
     for b in range(8):
         arrived(block_in.at[b], recv4.at[b])
-        both = jnp.concatenate([block_in[b], jnp.zeros((24, 256), jnp.float32)], axis=1)
+        both = jnp.concatenate(unpack(block_in[b, 0:8], block_in[b, 8:16], block_in[b, 16:18]), axis=0)
+        both = jnp.concatenate([jnp.where(lane < 96, both, 0.0), jnp.zeros((24, 256), jnp.float32)], axis=1)
         above = jnp.where(wide_lane < 48, both, 0.0)
         top = top + (pltpu.roll(above, 48 * b, 1) if b else above)
         below = both - above
@@ -206,36 +218,41 @@
         to = (2 * goal + c, column, rep)
         send_or_keep(rows_out.at[24 * c:24 * (c + 1)], out_ref.at[owner, :, columns], send5.at[c], recv5.at[far], to)
 
-    def place(half, i, j):
-        x, y = (pan + j, rep + i) if half == 0 else (pan + i, rep + j)
-        return x % 4, y % 4
+    def place(i, j):
+        return (pan + i * core + j * (1 - core)) % 4, (rep + i * (1 - core) + j * core) % 4
 
     def rows(half, i, j):
-        x, y = place(half, i, j)
+        x, y = place(i, j)
         return out_ref.at[block_at(x, z, half), :, pl.ds(pl.multiple_of(384 * y, 128), 384)]
 
     def to_neighbours(half, i):
         here = rows(half, i, 0)
+        if i == 2:
+            send(here, here, send8.at[half, 2], recv8.at[half, 2], (wide,) + place(0, 2))
         for way in (1, 3):
-            send(here, here, send7.at[half, way // 2, i], recv7.at[half, way // 2, i], (wide,) + place(half, 0, way))
+            send(here, here, send7.at[half, way // 2, i], recv7.at[half, way // 2, i], (wide,) + place(0, way))
 
     for half in range(2):
         here = rows(half, 0, 0)
         arrived(here, recv5.at[half])
-        for i in (1, 3, 2):
-            send(here, here, send6.at[half, i], recv6.at[half, 4 - i], (wide,) + place(half, i, 0))
+        for i in (2, 1, 3):
+            send(here, here, send6.at[half, i], recv6.at[half, 4 - i], (wide,) + place(i, 0))
         to_neighbours(half, 0)
         for i in (1, 3, 2):
             arrived(rows(half, i, 0), recv6.at[half, i])
             to_neighbours(half, i)
-        for i in (0, 1, 3, 2):
+        for i in (0, 1, 3):
             come, go = (1, 3) if i < 2 else (3, 1)
             here = rows(half, i, come)
             arrived(here, recv7.at[half, 1 if i < 2 else 0, i])
-            send(here, here, send8.at[half, i], recv8.at[half, i], (wide,) + place(half, 0, go))
+            send(here, here, send8.at[half, i], recv8.at[half, i], (wide,) + place(0, go))
     for half in range(2):
         for i in range(4):
-            arrived(rows(half, i, 3 if i < 2 else 1), recv7.at[half, 0 if i < 2 else 1, i])
+            if i != 2:
+                arrived(rows(half, i, 3 if i < 2 else 1), recv7.at[half, 0 if i < 2 else 1, i])
+            else:
+                arrived(rows(half, i, 3), recv7.at[half, 0, i])
+                arrived(rows(half, i, 1), recv7.at[half, 1, i])
             arrived(rows(half, i, 2), recv8.at[half, i])
 
     for args in sent:
@@ -264,8 +281,8 @@
             pltpu.VMEM((2, 4, 192, 128), jnp.float32),
             pltpu.VMEM((192, 384), jnp.float32),
             pltpu.VMEM((4, 48, 384), jnp.float32),
-            pltpu.VMEM((8, 24, 128), jnp.float32),
-            pltpu.VMEM((8, 24, 128), jnp.float32),
+            pltpu.VMEM((8, 18, 128), jnp.float32),
+            pltpu.VMEM((8, 18, 128), jnp.float32),
             pltpu.VMEM((48, 384), jnp.float32),
             dma((3,)), dma((2, 8)), dma((2, 8)),
             dma((4, 4)), dma((4, 4)), dma((4, 4)), dma((4, 4)), dma((4, 4)), dma((4, 4)),
@@ -275,6 +292,7 @@
         compiler_params=pltpu.CompilerParams(collective_id=0, has_side_effects=True, vmem_limit_bytes=24 * 1024 * 1024),
         cost_estimate=pl.CostEstimate(flops=60_000_000, bytes_accessed=2_000_000, transcendentals=0),
     )(*(pltpu.with_memory_space_constraint(operand, pltpu.HBM) for operand in (block_sizes, amplitudes, jnp.swapaxes(integrals, 1, 2))))
+    negated, pair_energies = lax.optimization_barrier((negated, pair_energies))
     row_start = lax.axis_index("wide") * 24
     energy_rows = lax.dynamic_slice_in_dim(pair_energies, row_start, 24, 1)
     update = negated / (energy_rows[:, :, None] + pair_energies[:, None, :])

time: 109 us -> 105 us (0.963)
  the two profiles are of different devices: /device:TPU:64 before, /device:TPU:56 now
where the time goes in v5:
time: 105 us
  Pallas kernels  103 us (98%)
  other arithmetic  1.61 us (2%)
    pallas_call x1, Pallas kernels, shards(): pl.pallas_call(cycle_kernel, out_shape=jax.ShapeDtypeStruct((8, 24, 1536)...  103 us

profile of v5, /device:TPU:56, one launch (start us, length us, event | category | flops | bytes accessed | tf_op | source)
XLA Modules:
  0.0 105.1 jit_solution(6378747145704113803)
XLA Ops:
  0.6 0.0 copy-start
  0.6 102.7 %shard_map.59 = f32[8,24,1536]{2,1,0:T(8,128)S(1)} custom-call(s32[8]{0:T(128)} %sizes_hbm.1, f32[8,24,96]{2,1,0:T(8,128)} %amp_hbm.1, f32[8,24,96]{2,1,0:T(8,128)} %bitcast.1), custom_call_target="tpu_custom_call" | custom-call | flops 60000000 | bytes 2000000 | tf_op jit(solution)/shard_map/pallas_call | solution.py:268
  103.4 0.0 copy-done
  103.4 0.1 constant_dynamic-slice_fusion
  103.5 1.6 %add_divide_fusion = (f32[8,24,1536]{2,1,0:T(8,128)}, f32[8,24,1536]{2,1,0:T(8,128)}) fusion(f32[8,24,1536]{2,1,0:T(8,128)S(1)} %shard_map.59, f32[8,1536]{1,0:T(8,128)S(1)} %copy-done, f32[8,24]{1,0:T(8,128)S(1)} %constant_dynamic-slice_fusion), kind=kLoop, calls=%fused_computation | loop fusion | flops 884736 | bytes 3588864 | tf_op jit(solution)/shard_map/div | solution.py:298
Async XLA Ops:
  0.6 102.7 %copy-start = (f32[8,1536]{1,0:T(8,128)S(1)}, f32[8,1536]{1,0:T(8,128)}, u32[]{:S(2)}) copy-start(f32[8,1536]{1,0:T(8,128)} %param.6) | copy-start | bytes 147460

commit v6 on v5

--- a/solution.py
+++ b/solution.py
@@ -65,9 +65,6 @@
         pltpu.make_async_copy(int_hbm, int_ref, load.at[1]),
         pltpu.make_async_copy(sizes_hbm, sizes_ref, load.at[2]),
     ]
-    for copy in loads:
-        copy.start()
-
     def block_at(x, at, far):
         one = (x + 4 - at % 4) % 4
         off = (4 * one + 2 + 32 - at) % 32
@@ -84,6 +81,8 @@
     barrier = pltpu.get_barrier_semaphore()
     for to in callers:
         pl.semaphore_signal(barrier, inc=1, device_id=device(*to), device_id_type=MESH)
+    for copy in loads:
+        copy.start()
 
     row_at = wide * 24 + lax.broadcasted_iota(jnp.int32, (24, 128), 0)
     lane = lax.broadcasted_iota(jnp.int32, (24, 128), 1)
@@ -122,26 +121,30 @@
     slot1 = (rank % 4) * 2 + core
     for step in (4, 3, 5, 2, 6, 1, 7, 0):
         h = (owner + step) % 8
+        to = (2 * (4 * h + rep) + rank // 4, pan, band)
+        send_or_keep(stage.at[1, h], int_packed.at[rank // 4, rep, slot1], send1.at[1, step], recv1.at[1, slot1], to)
+    for step in (4, 3, 5, 2, 6, 1, 7, 0):
+        h = (owner + step) % 8
         to = (2 * (4 * h + band) + rank // 4, pan, rep)
         send_or_keep(stage.at[0, h], amp_packed.at[rep, slot1], send1.at[0, step], recv1.at[0, slot1], to)
-        to = (2 * (4 * h + rep) + rank // 4, pan, band)
-        send_or_keep(stage.at[1, h], int_packed.at[rank // 4, rep, slot1], send1.at[1, step], recv1.at[1, slot1], to)
 
     sibling = (2 * z + 1 - core, pan, rep)
+    for pair in range(4):
+        two = slice(2 * pair, 2 * pair + 2)
+        for i in (2 * pair, 2 * pair + 1):
+            arrived(int_packed.at[core, layer, i], recv1.at[1, i])
+        here = int_packed.at[core, layer, two]
+        for step in (2, 1, 3):
+            to = (2 * (4 * owner + (layer + step) % 4) + core, pan, rep)
+            send(here, here, send_b.at[pair, step], recv_b.at[pair, layer], to)
+        send(here, here, send_c.at[pair, 0], recv_c.at[pair, layer], sibling)
     for pair in range(4):
         two = slice(2 * pair, 2 * pair + 2)
         for i in (2 * pair, 2 * pair + 1):
             arrived(amp_packed.at[rep, i], recv1.at[0, i])
         here = amp_packed.at[rep, two]
-        for step in range(1, 4):
+        for step in (2, 1, 3):
             send(here, here, send_a.at[pair, step], recv_a.at[pair, rep], (wide, pan, (rep + step) % 4))
-        for i in (2 * pair, 2 * pair + 1):
-            arrived(int_packed.at[core, layer, i], recv1.at[1, i])
-        here = int_packed.at[core, layer, two]
-        for step in range(1, 4):
-            to = (2 * (4 * owner + (layer + step) % 4) + core, pan, rep)
-            send(here, here, send_b.at[pair, step], recv_b.at[pair, layer], to)
-        send(here, here, send_c.at[pair, 0], recv_c.at[pair, layer], sibling)
 
     def spread(packed, whole, index, mask):
         for i in range(8):
@@ -149,24 +152,26 @@
             for row, value in zip((0, 8, 16), values):
                 whole[index + (slice(24 * i + row, 24 * i + row + 8),)] = jnp.where(lane8 < 96, value, 0.0) if mask else value
 
-    spread(amp_packed, amp_all, (rep,), True)
     spread(int_packed, int_all, (core, layer), False)
     for step in (1, 3, 2):
-        y, l = (rep + step) % 4, (layer + step) % 4
+        l = (layer + step) % 4
         for pair in range(4):
             two = slice(2 * pair, 2 * pair + 2)
-            arrived(int_packed.at[core, l, two], recv_b.at[pair, l])
             here = int_packed.at[core, l, two]
+            arrived(here, recv_b.at[pair, l])
             send(here, here, send_c.at[pair, step], recv_c.at[pair, l], sibling)
         spread(int_packed, int_all, (core, l), False)
-        for pair in range(4):
-            arrived(amp_packed.at[y, 2 * pair:2 * pair + 2], recv_a.at[pair, y])
-        spread(amp_packed, amp_all, (y,), True)
+    spread(amp_packed, amp_all, (rep,), True)
     for step in (0, 1, 3, 2):
         l = (layer + step) % 4
         for pair in range(4):
             arrived(int_packed.at[1 - core, l, 2 * pair:2 * pair + 2], recv_c.at[pair, l])
         spread(int_packed, int_all, (1 - core, l), False)
+    for step in (1, 3, 2):
+        y = (rep + step) % 4
+        for pair in range(4):
+            arrived(amp_packed.at[y, 2 * pair:2 * pair + 2], recv_a.at[pair, y])
+        spread(amp_packed, amp_all, (y,), True)
 
     for side in range(2):
         total = jnp.zeros((192, 192), jnp.float32)
@@ -176,7 +181,7 @@
                 (((1,), (1,)), ((), ())), precision=lax.Precision.HIGHEST, preferred_element_type=jnp.float32,
             )
         part[:, 192 * side:192 * (side + 1)] = total
-    for step in range(1, 4):
+    for step in (2, 1, 3):
         x = (pan + step) % 4
         rows = part.at[pl.ds(pl.multiple_of(48 * x, 8), 48)]
         send(rows, parts.at[pan], send3.at[step], recv3.at[pan], (wide, x, rep))

time: 105 us -> 103 us (0.981)
  Pallas kernels: 103 us -> 100 us
    pallas_call x1, Pallas kernels: 103 us -> 100 us  [shards(): pl.pallas_call(cycle_kernel, out_shape=jax.ShapeDtypeStruct((8, 24, 1536)...]
where the time goes in v6:
time: 103 us
  Pallas kernels  100 us (97%)
  other arithmetic  1.61 us (2%)
    pallas_call x1, Pallas kernels, shards(): pl.pallas_call(cycle_kernel, out_shape=jax.ShapeDtypeStruct((8, 24, 1536)...  100 us

profile of v6, /device:TPU:56, one launch (start us, length us, event | category | flops | bytes accessed | tf_op | source)
XLA Modules:
  0.0 102.7 jit_solution(9520456030080671851)
XLA Ops:
  0.6 0.0 copy-start
  0.6 100.3 %shard_map.59 = f32[8,24,1536]{2,1,0:T(8,128)S(1)} custom-call(s32[8]{0:T(128)} %sizes_hbm.1, f32[8,24,96]{2,1,0:T(8,128)} %amp_hbm.1, f32[8,24,96]{2,1,0:T(8,128)} %bitcast.1), custom_call_target="tpu_custom_call" | custom-call | flops 60000000 | bytes 2000000 | tf_op jit(solution)/shard_map/pallas_call | solution.py:273
  101.0 0.0 copy-done
  101.0 0.1 constant_dynamic-slice_fusion
  101.0 1.6 %add_divide_fusion = (f32[8,24,1536]{2,1,0:T(8,128)}, f32[8,24,1536]{2,1,0:T(8,128)}) fusion(f32[8,24,1536]{2,1,0:T(8,128)S(1)} %shard_map.59, f32[8,1536]{1,0:T(8,128)S(1)} %copy-done, f32[8,24]{1,0:T(8,128)S(1)} %constant_dynamic-slice_fusion), kind=kLoop, calls=%fused_computation | loop fusion | flops 884736 | bytes 3588864 | tf_op jit(solution)/shard_map/div | solution.py:303
Async XLA Ops:
  0.6 100.3 %copy-start = (f32[8,1536]{1,0:T(8,128)S(1)}, f32[8,1536]{1,0:T(8,128)}, u32[]{:S(2)}) copy-start(f32[8,1536]{1,0:T(8,128)} %param.6) | copy-start | bytes 147460

commit v7 on v6

--- a/solution.py
+++ b/solution.py
@@ -146,13 +146,20 @@
         for step in (2, 1, 3):
             send(here, here, send_a.at[pair, step], recv_a.at[pair, rep], (wide, pan, (rep + step) % 4))
 
-    def spread(packed, whole, index, mask):
+    def spread(packed, index, whole, to, start_row, mask):
         for i in range(8):
             values = unpack(*(packed[index + (i, slice(*rows))] for rows in ((0, 8), (8, 16), (16, 18))))
             for row, value in zip((0, 8, 16), values):
-                whole[index + (slice(24 * i + row, 24 * i + row + 8),)] = jnp.where(lane8 < 96, value, 0.0) if mask else value
-
-    spread(int_packed, int_all, (core, layer), False)
+                at = pl.ds(pl.multiple_of(start_row + 24 * i + row, 8), 8)
+                whole[to, at] = jnp.where(lane8 < 96, value, 0.0) if mask else value
+
+    def product(rows, y):
+        return lax.dot_general(
+            amp_all[y, rows], int_all[y], (((1,), (1,)), ((), ())),
+            precision=lax.Precision.HIGHEST, preferred_element_type=jnp.float32,
+        )
+
+    spread(int_packed, (core, layer), int_all, layer, 192 * core, False)
     for step in (1, 3, 2):
         l = (layer + step) % 4
         for pair in range(4):
@@ -160,31 +167,28 @@
             here = int_packed.at[core, l, two]
             arrived(here, recv_b.at[pair, l])
             send(here, here, send_c.at[pair, step], recv_c.at[pair, l], sibling)
-        spread(int_packed, int_all, (core, l), False)
-    spread(amp_packed, amp_all, (rep,), True)
+        spread(int_packed, (core, l), int_all, l, 192 * core, False)
+    spread(amp_packed, (rep,), amp_all, rep, 0, True)
     for step in (0, 1, 3, 2):
         l = (layer + step) % 4
         for pair in range(4):
             arrived(int_packed.at[1 - core, l, 2 * pair:2 * pair + 2], recv_c.at[pair, l])
-        spread(int_packed, int_all, (1 - core, l), False)
+        spread(int_packed, (1 - core, l), int_all, l, 192 * (1 - core), False)
+
+    part[...] = product(slice(None), rep)
     for step in (1, 3, 2):
         y = (rep + step) % 4
         for pair in range(4):
             arrived(amp_packed.at[y, 2 * pair:2 * pair + 2], recv_a.at[pair, y])
-        spread(amp_packed, amp_all, (y,), True)
-
-    for side in range(2):
-        total = jnp.zeros((192, 192), jnp.float32)
-        for y in range(4):
-            total = total + lax.dot_general(
-                amp_all[y], int_all[side, y],
-                (((1,), (1,)), ((), ())), precision=lax.Precision.HIGHEST, preferred_element_type=jnp.float32,
-            )
-        part[:, 192 * side:192 * (side + 1)] = total
-    for step in (2, 1, 3):
+        spread(amp_packed, (y,), amp_all, y, 0, True)
+        if step != 2:
+            part[...] += product(slice(None), y)
+    for step in (2, 1, 3, 0):
         x = (pan + step) % 4
-        rows = part.at[pl.ds(pl.multiple_of(48 * x, 8), 48)]
-        send(rows, parts.at[pan], send3.at[step], recv3.at[pan], (wide, x, rep))
+        rows = pl.ds(pl.multiple_of(48 * x, 8), 48)
+        part[rows] += product(rows, (rep + 2) % 4)
+        if step:
+            send(part.at[rows], parts.at[pan], send3.at[step], recv3.at[pan], (wide, x, rep))
     parts[pan] = part[pl.ds(pl.multiple_of(48 * pan, 8), 48)]
     for step in range(1, 4):
         x = (pan + step) % 4
@@ -283,7 +287,7 @@
             pltpu.VMEM((4, 8, 18, 128), jnp.float32),
             pltpu.VMEM((2, 4, 8, 18, 128), jnp.float32),
             pltpu.VMEM((4, 192, 128), jnp.float32),
-            pltpu.VMEM((2, 4, 192, 128), jnp.float32),
+            pltpu.VMEM((4, 384, 128), jnp.float32),
             pltpu.VMEM((192, 384), jnp.float32),
             pltpu.VMEM((4, 48, 384), jnp.float32),
             pltpu.VMEM((8, 18, 128), jnp.float32),

time: 103 us -> 103 us (level)
  the two profiles are of different devices: /device:TPU:56 before, /device:TPU:32 now
where the time goes in v7:
time: 103 us; the launch traced here: 102 us
  Pallas kernels  100 us (97%)
  other arithmetic  1.61 us (2%)
    pallas_call x1, Pallas kernels, shards(): pl.pallas_call(cycle_kernel, out_shape=jax.ShapeDtypeStruct((8, 24, 1536)...  100 us

profile of v7, /device:TPU:32, one launch (start us, length us, event | category | flops | bytes accessed | tf_op | source)
XLA Modules:
  0.0 102.3 jit_solution(741142472399210857)
XLA Ops:
  0.6 0.0 copy-start
  0.6 100.0 %shard_map.59 = f32[8,24,1536]{2,1,0:T(8,128)S(1)} custom-call(s32[8]{0:T(128)} %sizes_hbm.1, f32[8,24,96]{2,1,0:T(8,128)} %amp_hbm.1, f32[8,24,96]{2,1,0:T(8,128)} %bitcast.1), custom_call_target="tpu_custom_call" | custom-call | flops 60000000 | bytes 2000000 | tf_op jit(solution)/shard_map/pallas_call | solution.py:277
  100.6 0.0 copy-done
  100.6 0.1 constant_dynamic-slice_fusion
  100.7 1.6 %add_divide_fusion = (f32[8,24,1536]{2,1,0:T(8,128)}, f32[8,24,1536]{2,1,0:T(8,128)}) fusion(f32[8,24,1536]{2,1,0:T(8,128)S(1)} %shard_map.59, f32[8,1536]{1,0:T(8,128)S(1)} %copy-done, f32[8,24]{1,0:T(8,128)S(1)} %constant_dynamic-slice_fusion), kind=kLoop, calls=%fused_computation | loop fusion | flops 884736 | bytes 3588864 | tf_op jit(solution)/shard_map/div | solution.py:307
Async XLA Ops:
  0.6 100.0 %copy-start = (f32[8,1536]{1,0:T(8,128)S(1)}, f32[8,1536]{1,0:T(8,128)}, u32[]{:S(2)}) copy-start(f32[8,1536]{1,0:T(8,128)} %param.6) | copy-start | bytes 147460

commit v8 on v7

--- a/solution.py
+++ b/solution.py
@@ -46,6 +46,11 @@
         @pl.when(jnp.logical_not(is_me(to)))
         def _():
             remote(src, dst, ssem, rsem, to).wait_send()
+
+    def drain(list_of_sends, finish):
+        for args in list_of_sends:
+            finish(*args)
+        list_of_sends.clear()
 
     def arrived(dst, rsem):
         pltpu.make_async_copy(dst, dst, rsem).wait()
@@ -220,12 +225,18 @@
     rows_out[24:48] = -(cycle[24:48] + bottom)
 
     columns = pl.ds(pl.multiple_of(384 * rep, 128), 384)
+    earlier, earlier_or_kept = sent[:], sent_or_kept[:]
+    sent.clear()
+    sent_or_kept.clear()
     goal = 8 * layer + 4 * core + pan
     column = (owner + pan) % 4
     far = ((owner + 8 - block_at(column, goal, 0)) % 8) // 4
     for c in range(2):
         to = (2 * goal + c, column, rep)
         send_or_keep(rows_out.at[24 * c:24 * (c + 1)], out_ref.at[owner, :, columns], send5.at[c], recv5.at[far], to)
+
+    drain(earlier, lambda *args: remote(*args).wait_send())
+    drain(earlier_or_kept, finish_send)
 
     def place(i, j):
         return (pan + i * core + j * (1 - core)) % 4, (rep + i * (1 - core) + j * core) % 4
@@ -255,6 +266,11 @@
             here = rows(half, i, come)
             arrived(here, recv7.at[half, 1 if i < 2 else 0, i])
             send(here, here, send8.at[half, i], recv8.at[half, i], (wide,) + place(0, go))
+        if half == 0:
+            near_sends = sent[:]
+            sent.clear()
+    drain(near_sends, lambda *args: remote(*args).wait_send())
+    drain(sent_or_kept, finish_send)
     for half in range(2):
         for i in range(4):
             if i != 2:
@@ -264,10 +280,7 @@
                 arrived(rows(half, i, 1), recv7.at[half, 1, i])
             arrived(rows(half, i, 2), recv8.at[half, i])
 
-    for args in sent:
-        remote(*args).wait_send()
-    for args in sent_or_kept:
-        finish_send(*args)
+    drain(sent, lambda *args: remote(*args).wait_send())
 
 
 def shards(amplitudes, integrals, pair_energies, block_sizes):

time: 103 us -> 102 us (level)
  no operation moved by 1% of the time
where the time goes in v8:
time: 102 us
  Pallas kernels  99.8 us (98%)
  other arithmetic  1.61 us (2%)
    pallas_call x1, Pallas kernels, shards(): pl.pallas_call(cycle_kernel, out_shape=jax.ShapeDtypeStruct((8, 24, 1536)...  99.8 us

profile of v8, /device:TPU:32, one launch (start us, length us, event | category | flops | bytes accessed | tf_op | source)
XLA Modules:
  0.0 102.1 jit_solution(7474227951237580760)
XLA Ops:
  0.6 0.0 copy-start
  0.6 99.8 %shard_map.59 = f32[8,24,1536]{2,1,0:T(8,128)S(1)} custom-call(s32[8]{0:T(128)} %sizes_hbm.1, f32[8,24,96]{2,1,0:T(8,128)} %amp_hbm.1, f32[8,24,96]{2,1,0:T(8,128)} %bitcast.1), custom_call_target="tpu_custom_call" | custom-call | flops 60000000 | bytes 2000000 | tf_op jit(solution)/shard_map/pallas_call | solution.py:290
  100.4 0.0 copy-done
  100.5 0.1 constant_dynamic-slice_fusion
  100.5 1.6 %add_divide_fusion = (f32[8,24,1536]{2,1,0:T(8,128)}, f32[8,24,1536]{2,1,0:T(8,128)}) fusion(f32[8,24,1536]{2,1,0:T(8,128)S(1)} %shard_map.59, f32[8,1536]{1,0:T(8,128)S(1)} %copy-done, f32[8,24]{1,0:T(8,128)S(1)} %constant_dynamic-slice_fusion), kind=kLoop, calls=%fused_computation | loop fusion | flops 884736 | bytes 3588864 | tf_op jit(solution)/shard_map/div | solution.py:320
Async XLA Ops:
  0.6 99.8 %copy-start = (f32[8,1536]{1,0:T(8,128)S(1)}, f32[8,1536]{1,0:T(8,128)}, u32[]{:S(2)}) copy-start(f32[8,1536]{1,0:T(8,128)} %param.6) | copy-start | bytes 147460

commit v9 on v8

--- a/solution.py
+++ b/solution.py
@@ -245,10 +245,13 @@
         x, y = place(i, j)
         return out_ref.at[block_at(x, z, half), :, pl.ds(pl.multiple_of(384 * y, 128), 384)]
 
+    def straight(half, i):
+        return i == 2 or (half == 1 and i > 0)
+
     def to_neighbours(half, i):
         here = rows(half, i, 0)
-        if i == 2:
-            send(here, here, send8.at[half, 2], recv8.at[half, 2], (wide,) + place(0, 2))
+        if straight(half, i):
+            send(here, here, send8.at[half, i], recv8.at[half, i], (wide,) + place(0, 2))
         for way in (1, 3):
             send(here, here, send7.at[half, way // 2, i], recv7.at[half, way // 2, i], (wide,) + place(0, way))
 
@@ -261,7 +264,7 @@
         for i in (1, 3, 2):
             arrived(rows(half, i, 0), recv6.at[half, i])
             to_neighbours(half, i)
-        for i in (0, 1, 3):
+        for i in (0,) if half else (0, 1, 3):
             come, go = (1, 3) if i < 2 else (3, 1)
             here = rows(half, i, come)
             arrived(here, recv7.at[half, 1 if i < 2 else 0, i])
@@ -273,7 +276,7 @@
     drain(sent_or_kept, finish_send)
     for half in range(2):
         for i in range(4):
-            if i != 2:
+            if not straight(half, i):
                 arrived(rows(half, i, 3 if i < 2 else 1), recv7.at[half, 0 if i < 2 else 1, i])
             else:
                 arrived(rows(half, i, 3), recv7.at[half, 0, i])

time: 102 us -> 100 us (0.980)
  the two profiles are of different devices: /device:TPU:32 before, /device:TPU:1 now
where the time goes in v9:
time: 100 us; the launch traced here: 98.4 us
  Pallas kernels  96 us (96%)
  other arithmetic  1.61 us (2%)
    pallas_call x1, Pallas kernels, shards(): pl.pallas_call(cycle_kernel, out_shape=jax.ShapeDtypeStruct((8, 24, 1536)...  96 us

profile of v9, /device:TPU:1, one launch (start us, length us, event | category | flops | bytes accessed | tf_op | source)
XLA Modules:
  0.0 98.4 jit_solution(11087255572815562754)
XLA Ops:
  0.6 0.0 copy-start
  0.6 96.0 %shard_map.59 = f32[8,24,1536]{2,1,0:T(8,128)S(1)} custom-call(s32[8]{0:T(128)} %sizes_hbm.1, f32[8,24,96]{2,1,0:T(8,128)} %amp_hbm.1, f32[8,24,96]{2,1,0:T(8,128)} %bitcast.1), custom_call_target="tpu_custom_call" | custom-call | flops 60000000 | bytes 2000000 | tf_op jit(solution)/shard_map/pallas_call | solution.py:293
  96.7 0.0 copy-done
  96.7 0.1 constant_dynamic-slice_fusion
  96.8 1.6 %add_divide_fusion = (f32[8,24,1536]{2,1,0:T(8,128)}, f32[8,24,1536]{2,1,0:T(8,128)}) fusion(f32[8,24,1536]{2,1,0:T(8,128)S(1)} %shard_map.59, f32[8,1536]{1,0:T(8,128)S(1)} %copy-done, f32[8,24]{1,0:T(8,128)S(1)} %constant_dynamic-slice_fusion), kind=kLoop, calls=%fused_computation | loop fusion | flops 884736 | bytes 3588864 | tf_op jit(solution)/shard_map/div | solution.py:323
Async XLA Ops:
  0.6 96.1 %copy-start = (f32[8,1536]{1,0:T(8,128)S(1)}, f32[8,1536]{1,0:T(8,128)}, u32[]{:S(2)}) copy-start(f32[8,1536]{1,0:T(8,128)} %param.6) | copy-start | bytes 147460

commit v10 on v9

--- a/solution.py
+++ b/solution.py
@@ -246,7 +246,7 @@
         return out_ref.at[block_at(x, z, half), :, pl.ds(pl.multiple_of(384 * y, 128), 384)]
 
     def straight(half, i):
-        return i == 2 or (half == 1 and i > 0)
+        return i > 0
 
     def to_neighbours(half, i):
         here = rows(half, i, 0)
@@ -264,7 +264,7 @@
         for i in (1, 3, 2):
             arrived(rows(half, i, 0), recv6.at[half, i])
             to_neighbours(half, i)
-        for i in (0,) if half else (0, 1, 3):
+        for i in (0,):
             come, go = (1, 3) if i < 2 else (3, 1)
             here = rows(half, i, come)
             arrived(here, recv7.at[half, 1 if i < 2 else 0, i])

time: 100 us -> 99.9 us (level); the launches traced: 98.4 us -> 99.7 us
  Pallas kernels: 96 us -> 97.4 us
    pallas_call x1, Pallas kernels: 96 us -> 97.4 us  [shards(): pl.pallas_call(cycle_kernel, out_shape=jax.ShapeDtypeStruct((8, 24, 1536)...]
where the time goes in v10:
time: 99.9 us; the launch traced here: 99.7 us
  Pallas kernels  97.4 us (97%)
  other arithmetic  1.61 us (2%)
    pallas_call x1, Pallas kernels, shards(): pl.pallas_call(cycle_kernel, out_shape=jax.ShapeDtypeStruct((8, 24, 1536)...  97.4 us

profile of v10, /device:TPU:1, one launch (start us, length us, event | category | flops | bytes accessed | tf_op | source)
XLA Modules:
  0.0 99.7 jit_solution(7736929811203330956)
XLA Ops:
  0.6 0.0 copy-start
  0.6 97.4 %shard_map.59 = f32[8,24,1536]{2,1,0:T(8,128)S(1)} custom-call(s32[8]{0:T(128)} %sizes_hbm.1, f32[8,24,96]{2,1,0:T(8,128)} %amp_hbm.1, f32[8,24,96]{2,1,0:T(8,128)} %bitcast.1), custom_call_target="tpu_custom_call" | custom-call | flops 60000000 | bytes 2000000 | tf_op jit(solution)/shard_map/pallas_call | solution.py:293
  98.0 0.0 copy-done
  98.1 0.1 constant_dynamic-slice_fusion
  98.1 1.6 %add_divide_fusion = (f32[8,24,1536]{2,1,0:T(8,128)}, f32[8,24,1536]{2,1,0:T(8,128)}) fusion(f32[8,24,1536]{2,1,0:T(8,128)S(1)} %shard_map.59, f32[8,1536]{1,0:T(8,128)S(1)} %copy-done, f32[8,24]{1,0:T(8,128)S(1)} %constant_dynamic-slice_fusion), kind=kLoop, calls=%fused_computation | loop fusion | flops 884736 | bytes 3588864 | tf_op jit(solution)/shard_map/div | solution.py:323
Async XLA Ops:
  0.6 97.4 %copy-start = (f32[8,1536]{1,0:T(8,128)S(1)}, f32[8,1536]{1,0:T(8,128)}, u32[]{:S(2)}) copy-start(f32[8,1536]{1,0:T(8,128)} %param.6) | copy-start | bytes 147460
